TPU v7x, 32 devices: a whole 2x2x4 slice. The times are simulated.
32 devices in a mesh: expert: 16 (over z, y, x), dp: 2 (over core).
Axes of the slice: x: 2, y: 2, z: 4, core: 2. Of those that a mesh axis runs over, the one named last changes fastest.
Arguments:
- expert_ids: int32 [4096, 8], P(('expert', 'dp')), may hold values from 0 to 15, all different within a row; in each aligned block of 128 rows (0 to 127, 128 to 255, ...) at most 80 rows name the same one
- gates: float32 [4096, 8], P(('expert', 'dp')), may hold values from 0.05 to 1
- hidden: bfloat16 [16, 2560, 768], P('expert', 'dp'), may hold values from -6 to 6
- weight: bfloat16 [16, 768, 2048], P('expert'), may hold values from -0.21875 to 0.21875
- out_grad: bfloat16 [4096, 2048], P(('expert', 'dp')), may hold values from -6 to 6
Outputs:
- combined: bfloat16 [4096, 2048], P(('expert', 'dp'))
- gate_grads: float32 [4096, 8], P(('expert', 'dp'))
- hidden_grads: bfloat16 [16, 2560, 768], P('expert', 'dp')
- weight_grads: bfloat16 [16, 768, 2048], P('expert', None, 'dp')
Inputs may be any that keep to these rules, and one draw needn't show every extreme that they name: `expert_ids`: each token names 8 different experts; among the 128 tokens of one device no expert is named more than 80 times, a bound that some block reaches.
All inputs are finite; a program needn't handle non-finite values.
Results may differ from a plain program's by a relative error of at most 0.0049.
Values may be sent and summed in bfloat16 or wider, within the bound.
No kernel may reach another device: no remote copies, remote signals or barrier semaphores. Data moves between devices by JAX's collectives and lax.ppermute only.
A program may use at most 128 MiB of HBM per device.

v0:
```python
import functools

import jax
import jax.numpy as jnp
from jax import lax
from jax.experimental import pallas as pl
from jax.experimental.pallas import tpu as pltpu
from jax.sharding import PartitionSpec as P

F32 = jnp.float32
BF16 = jnp.bfloat16
VMEM_BYTES = 16 * 1024 * 1024
COST = 1024
NEAR_COST = 10**10


def call(body, name, grid, in_specs, out_specs, out_shape, scalars, operands, scratch=(), aliases=None, room=1, cost=COST):
    return pl.pallas_call(
        body,
        name=name,
        grid_spec=pltpu.PrefetchScalarGridSpec(
            num_scalar_prefetch=1, grid=grid, in_specs=in_specs, out_specs=out_specs, scratch_shapes=scratch
        ),
        out_shape=out_shape,
        input_output_aliases=aliases or {},
        cost_estimate=pl.CostEstimate(flops=cost, bytes_accessed=COST, transcendentals=0),
        compiler_params=pltpu.CompilerParams(vmem_limit_bytes=room * VMEM_BYTES),
    )(scalars, *operands)


def direct(body, name, out_shape, scalars, operands, out_specs=None, scratch=(), aliases=None, places=None, room=1):
    places = places or {}
    vmem, smem = pl.BlockSpec(memory_space=pltpu.VMEM), pl.BlockSpec(memory_space=pltpu.SMEM)
    several = isinstance(out_shape, (list, tuple))
    return pl.pallas_call(
        body,
        name=name,
        in_specs=[smem] + [places.get(at, vmem) for at in range(len(operands))],
        out_specs=out_specs or ([vmem] * len(out_shape) if several else vmem),
        out_shape=out_shape,
        scratch_shapes=scratch,
        input_output_aliases=aliases or {},
        cost_estimate=pl.CostEstimate(flops=COST, bytes_accessed=COST, transcendentals=0),
        compiler_params=pltpu.CompilerParams(vmem_limit_bytes=int(room * VMEM_BYTES)),
    )(scalars, *operands)


def follow(value, *earlier):
    anywhere = pl.BlockSpec(memory_space=pl.ANY)
    return pl.pallas_call(
        lambda *refs: None,
        name="follow",
        grid=(1,),
        in_specs=[anywhere] + [pl.BlockSpec((16, 128), lambda i: (0, 0))] * len(earlier),
        out_specs=anywhere,
        out_shape=jax.ShapeDtypeStruct(value.shape, value.dtype),
        input_output_aliases={0: 0},
        cost_estimate=pl.CostEstimate(flops=COST, bytes_accessed=COST, transcendentals=0),
        compiler_params=pltpu.CompilerParams(vmem_limit_bytes=VMEM_BYTES),
    )(value, *earlier)


def pieces_of(value):
    high = value.astype(BF16).astype(F32)
    middle = (value - high).astype(BF16).astype(F32)
    return high, middle, value - high - middle


def pack_body(meta, ids, gates, grad, out):
    width, tokens = grad.shape[1], grad.shape[0]
    extent = out.shape[1] - width
    count = meta[6]
    expert = lax.broadcasted_iota(jnp.int32, (extent, tokens), 0)
    piece = jnp.zeros((extent, tokens), jnp.int32)
    for number in range(1, 4):
        piece = piece + jnp.where(expert >= number * count, 1, 0)
    local = expert - piece * count
    named = jnp.zeros((extent, tokens), F32)
    gate = jnp.zeros((extent, tokens), F32)
    for choice in range(ids.shape[0]):
        hit = ids[choice : choice + 1, :] == local
        named = named + jnp.where(hit, 1.0, 0.0)
        gate = gate + jnp.where(hit, gates[choice : choice + 1, :], 0.0)
    before = lax.broadcasted_iota(jnp.int32, (tokens, tokens), 0) < lax.broadcasted_iota(jnp.int32, (tokens, tokens), 1)
    earlier = jnp.dot(named.astype(BF16), jnp.where(before, 1.0, 0.0).astype(BF16), preferred_element_type=F32)
    place = jnp.where(named > 0.0, earlier + meta[2].astype(F32), -1.0)
    high, middle, low = pieces_of(gate)
    table = jnp.where(piece == 0, place, jnp.where(piece == 1, high, jnp.where(piece == 2, middle, low)))
    out[:, :width] = grad[...]
    out[:, width:] = table.T.astype(BF16)


def collect_body(number, meta, *refs):
    tables, sides, outs = refs[:number], (refs[number : 2 * number], refs[2 * number : 3 * number]), refs[-2:]
    tokens = tables[0].shape[0]
    for side, out in zip(sides, outs):
        large = side[0].shape[1]
        for k in range(number):
            out[k * tokens : (k + 1) * tokens, :large] = side[k][...]
            out[k * tokens : (k + 1) * tokens, large:] = tables[k][...]


def forward_body(meta, hidden, weight, out):
    rows = hidden[:, 0].reshape(out.shape[0], hidden.shape[3])
    out[...] = jnp.dot(rows, weight[...], preferred_element_type=F32).astype(BF16)


def forward_first_body(peers, meta, hidden, weight, *refs):
    outs, (rows, matrix, sems) = refs[: len(peers)], refs[len(peers) :]
    tile = matrix.shape[2]
    copies = []
    for at, peer in enumerate(peers):
        part = hidden.at[:, lax.bitwise_xor(meta[0], peer)]
        copies.append(pltpu.make_async_copy(part, rows.at[at], sems.at[at]))
    for at in range(matrix.shape[0]):
        part = weight.at[:, at * tile : (at + 1) * tile]
        copies.append(pltpu.make_async_copy(part, matrix.at[at], sems.at[len(peers) + at]))
    for copy in copies:
        copy.start()
    for copy in copies[: len(peers)]:
        copy.wait()
    length = outs[0].shape[0]
    value = rows[...].reshape(len(peers) * length, rows.shape[3])
    for at in range(matrix.shape[0]):
        copies[len(peers) + at].wait()
        product = jnp.dot(value, matrix[at], preferred_element_type=F32).astype(BF16)
        for number, out in enumerate(outs):
            out[:, at * tile : (at + 1) * tile] = product[number * length : (number + 1) * length]


def turn_body(meta, hidden, after, out, final, final_turned):
    value = hidden[:, 0].reshape(final.shape)
    out[0] = value.T
    final[...] = value
    final_turned[...] = value.T


def turn_other_body(meta, hidden, out):
    out[...] = hidden[...].T


def selection(table, count, expert, rows):
    place = table[pl.ds(expert, 1), :]
    gate = table[pl.ds(expert + count, 1), :] + table[pl.ds(expert + 2 * count, 1), :]
    gate = gate + table[pl.ds(expert + 3 * count, 1), :]
    row = lax.broadcasted_iota(jnp.int32, (rows, place.shape[1]), 0).astype(F32)
    return row == place, gate


def grad_rows_body(plan, jobs, count, groups, meta, *refs):
    number = jobs * groups
    tables, tokens, outs, table = refs[:number], refs[number : 2 * number], refs[-1 - len(plan) : -1], refs[-1]
    rows = outs[0].shape[0] // len(plan[0][1]) // groups
    for job in range(jobs):
        asked = [(out, peer, parts.index(job)) for out, (peer, parts) in zip(outs, plan) if job in parts]
        for group in range(groups):
            table[...] = tables[job * groups + group][...].astype(F32).T
            choices, row_gates = [], []
            for _, peer, _ in asked:
                match, gate = selection(table, count, lax.bitwise_xor(meta[3], peer), rows)
                choices.append(jnp.where(match, 1.0, 0.0))
                row_gates.append(jnp.sum(jnp.where(match, gate, 0.0), 1, keepdims=True))
            choice = jnp.concatenate(choices, 0).astype(BF16)
            picked = jnp.dot(choice, tokens[job * groups + group][...], preferred_element_type=F32)
            value = (picked * jnp.concatenate(row_gates, 0)).astype(BF16)
            place = pl.multiple_of(lax.bitwise_xor(meta[1], group) * rows, rows)
            for at, (out, _, part) in enumerate(asked):
                out[pl.ds(place + part * groups * rows, rows), :] = value[at * rows : (at + 1) * rows]


def combine_body(peers, count, number, meta, *refs):
    packed, tokens, returned = refs[:number], refs[number : 2 * number], refs[2 * number + 1 : 2 * number + 1 + peers]
    part, table, weights, marks, inner = refs[-5:]
    rows, length = returned[0].shape[0], tokens[0].shape[0]
    step, last = pl.program_id(1), pl.num_programs(1) - 1

    def chosen(options):
        value = options[0][...]
        for at in range(1, number):
            value = jnp.where(pl.program_id(0) == at, options[at][...], value)
        return value

    @pl.when(step == 0)
    def _():
        inner[...] = jnp.zeros(inner.shape, F32)
        table[...] = chosen(packed).astype(F32).T
        highs, lows = [], []
        for peer in range(peers):
            match, gate = selection(table, count, lax.bitwise_xor(meta[3], peer), rows)
            high = gate.astype(BF16).astype(F32)
            marks[pl.ds(peer * rows, rows), :] = jnp.where(match, 1.0, 0.0)
            highs.append(jnp.where(match, high, 0.0))
            lows.append(jnp.where(match, gate - high, 0.0))
        weights[:length, :] = jnp.concatenate(highs, 0).T.astype(BF16)
        weights[length:, :] = jnp.concatenate(lows, 0).T.astype(BF16)

    @pl.when(step < last)
    def _():
        value = jnp.concatenate([ref[...] for ref in returned], 0)
        chunk = min(512, value.shape[1])
        for start in range(0, value.shape[1], chunk):
            total = jnp.dot(weights[...], value[:, start : start + chunk], preferred_element_type=F32)
            part[:, start : start + chunk] = (total[:length] + total[length:]).astype(part.dtype)
        products = lax.dot_general(value, chosen(tokens), (((1,), (1,)), ((), ())), preferred_element_type=F32)
        products = products * marks[...]
        for peer in range(peers):
            inner[peer : peer + 1, :] += jnp.sum(products[peer * rows : (peer + 1) * rows], 0, keepdims=True)

    @pl.when(step == last)
    def _():
        extent = -(-3 * count // 128) * 128
        row = lax.broadcasted_iota(jnp.int32, (extent, length), 0)
        placed = jnp.zeros((extent, length), F32)
        for at, piece in enumerate(pieces_of(inner[...])):
            for peer in range(peers):
                place = at * count + lax.bitwise_xor(meta[3], peer)
                placed = jnp.where(row == place, piece[peer : peer + 1, :], placed)
        part[:, :extent] = placed.T.astype(part.dtype)


def inside_body(plan, meta, weight, *refs):
    number = 1 + max(at for _, parts in plan for at, _ in parts)
    rows, out, token, (store, sems) = refs[:number], refs[-4], refs[-3], refs[-2:]
    shape = store.shape[1:]
    length, large = shape[0] * shape[1], weight.shape[1] // 2
    contract = (((1,), (1,)), ((), ()))
    copies = []
    for at, (peer, parts) in enumerate(plan):
        value = jnp.zeros((length, weight.shape[0]), F32)
        for half, (operand, start) in enumerate(parts):
            columns = pl.ds(pl.multiple_of(lax.bitwise_xor(1 - meta[4], half) * large, large), large)
            part = rows[operand][start : start + length, :]
            value = value + lax.dot_general(part, weight[:, columns], contract, preferred_element_type=F32)
        store[at] = value.astype(BF16).reshape(shape)
        copies.append(pltpu.make_async_copy(store.at[at], out.at[:, lax.bitwise_xor(meta[0], peer)], sems.at[at]))
        copies[-1].start()
    token[...] = jnp.zeros(token.shape, F32)
    for copy in copies:
        copy.wait()


def weight_grad_body(plan, number, half, meta, turned, *refs):
    rows, others, own = refs[:number], refs[-half - 1 : -1], refs[-1]
    length, tile = turned.shape[2], others[0].shape[1]

    def value_of(side, at):
        value = jnp.zeros((turned.shape[1], tile), F32)
        for peer, parts in plan:
            operand, start = parts[side]
            part = rows[operand][start : start + length, at * tile : (at + 1) * tile]
            value = value + jnp.dot(turned[peer], part, preferred_element_type=F32)
        return value

    for at in range(half):
        others[at][...] = value_of(0, at).astype(BF16)
        own[:, at * tile : (at + 1) * tile] = value_of(1, at)


def last_body(half, meta, turned, rows, turned_other, rows_other, earlier, *refs):
    others, grads = refs[:half], refs[-1]
    tile = others[0].shape[1]
    for at in range(half):
        columns = slice(at * tile, (at + 1) * tile)
        value = jnp.dot(turned[...], rows[:, columns], preferred_element_type=F32)
        value = value + jnp.dot(turned_other[...], rows_other[:, columns], preferred_element_type=F32)
        grads[:, columns] = (value + earlier[:, columns] + others[at][...].astype(F32)).astype(BF16)


def finish_body(count, meta, ids, kept, arrived, combined, gate_grads):
    width = combined.shape[1]
    combined[...] = (kept[:, :width] + arrived[:, :width].astype(F32)).astype(BF16)
    pieces = (kept[:, width:] + arrived[:, width:].astype(F32)).T
    inner = pieces[:count] + pieces[count : 2 * count] + pieces[2 * count : 3 * count]
    named = ids[...]
    found = jnp.zeros(gate_grads.shape, F32)
    for expert in range(count):
        found = found + jnp.where(named == expert, inner[expert : expert + 1, :], 0.0)
    gate_grads[...] = found


def per_device(expert_ids, gates, hidden, weight, out_grad):
    count = lax.axis_size("expert")
    peers = 1 << ((count.bit_length() - 1) // 2)
    planes = count // peers
    tokens, top = expert_ids.shape
    cap = hidden.shape[1] // count
    width, inside = out_grad.shape[1], hidden.shape[2]
    fold = 1
    while fold * cap % 16:
        fold *= 2
    groups = planes // fold
    group_rows, group_tokens = fold * cap, fold * tokens
    rows = planes * cap
    tile = min(512, width // 2)
    steps = width // tile
    half = steps // 2
    large = width // 2
    room = 1 if fold == 1 else 3
    last = peers - 1
    anywhere = pl.BlockSpec(memory_space=pl.ANY)
    glance = pl.BlockSpec((16, 128), lambda *i: (0, 0))

    me = lax.axis_index("expert")
    core = lax.axis_index("dp")
    column, plane = me % peers, me // peers
    meta = jnp.stack([column, plane // fold, (plane % fold) * cap, me, core, plane, count]).astype(jnp.int32)

    def swap(value, distance):
        return lax.ppermute(value, "expert", [(e, e ^ distance) for e in range(count)])

    def exchange(value):
        return lax.ppermute(value, "dp", [(0, 1), (1, 0)])

    matrix = weight[0]
    if fold == 1:
        blocks = hidden.reshape(planes, peers, cap, inside)
    else:
        blocks = hidden.reshape(planes, peers, cap, inside).transpose(1, 0, 2, 3).reshape(1, peers, rows, inside)
    block = (blocks.shape[0], 1, blocks.shape[2], inside)

    ids_turned = expert_ids.T
    extent = -(-4 * count // 128) * 128
    short = pl.BlockSpec((top, tokens), lambda i, m: (0, 0))
    relay = peers == 4 and fold == 1
    packed = call(
        pack_body, "pack", (1,),
        [short, short, pl.BlockSpec((tokens, width), lambda i, m: (0, 0))],
        pl.BlockSpec((tokens, width + extent), lambda i, m: (0, 0)),
        jax.ShapeDtypeStruct((tokens, width + extent), BF16),
        meta, (ids_turned, gates.T, out_grad),
        room=room,
    )
    gathered = [packed]
    for k in range(1, planes):
        if k & (k - 1) == 0:
            gathered.append(swap(packed, peers * k))
        else:
            gathered.append(None)
    early = [gathered[1 << k] for k in range((planes - 1).bit_length())]

    def forward(peer, after):
        return call(
            lambda meta, *refs: forward_body(meta, refs[0], refs[1], refs[-1]), f"forward{peer}", (steps,),
            [
                pl.BlockSpec(block, lambda i, m: (0, lax.bitwise_xor(m[0], peer), 0, 0)),
                pl.BlockSpec((inside, tile), lambda i, m: (0, i)),
            ]
            + [glance] * len(after),
            pl.BlockSpec((rows, tile), lambda i, m: (0, i)),
            jax.ShapeDtypeStruct((rows, width), BF16),
            meta, (blocks, matrix, *after),
        )

    outputs, after = {}, ()
    if relay:
        outputs[1], outputs[2] = direct(
            functools.partial(forward_first_body, (1, 2)), "forward1", [jax.ShapeDtypeStruct((rows, width), BF16)] * 2,
            meta, (blocks, matrix),
            scratch=[
                pltpu.VMEM((2, planes, cap, inside), BF16),
                pltpu.VMEM((steps, inside, tile), BF16),
                pltpu.SemaphoreType.DMA((2 + steps,)),
            ],
            places={0: anywhere, 1: anywhere}, room=3.75,
        )
        after = (outputs[2], packed)
    for peer in [peer for peer in list(range(1, peers)) + [0] if peer not in outputs]:
        outputs[peer] = forward(peer, after)
        after = (outputs[peer], packed)
    returned = [outputs[0]] + [swap(outputs[peer], peer) for peer in range(1, last)]
    turned, hidden_last, turned_last = call(
        turn_body, "turn", (peers,),
        [pl.BlockSpec(block, lambda i, m: (0, lax.bitwise_xor(m[0], i), 0, 0)), glance],
        [pl.BlockSpec((1, inside, rows), lambda i, m: (i, 0, 0)), pl.BlockSpec((rows, inside), lambda i, m: (0, 0)),
         pl.BlockSpec((inside, rows), lambda i, m: (0, 0))],
        [
            jax.ShapeDtypeStruct((peers, inside, rows), BF16), jax.ShapeDtypeStruct((rows, inside), BF16),
            jax.ShapeDtypeStruct((inside, rows), BF16),
        ],
        meta, (blocks, outputs[0]),
    )

    turned_other = call(
        turn_other_body, "turn_other", (1,),
        [pl.BlockSpec((rows, inside), lambda i, m: (0, 0))],
        pl.BlockSpec((inside, rows), lambda i, m: (0, 0)),
        jax.ShapeDtypeStruct((inside, rows), BF16),
        meta, (exchange(hidden_last),),
    )
    final_output = follow(outputs[last], *returned[:0:-1], turned_other, *early)
    returned.append(swap(final_output, last))
    for k in range(1, planes):
        lowest = k & -k
        if k != lowest:
            forwarded = gathered[k ^ lowest]
            forwarded = follow(forwarded, final_output) if relay else forwarded
            gathered[k] = swap(forwarded, peers * lowest)
    if fold > 1:
        gathered = [jnp.concatenate(gathered[g * fold : (g + 1) * fold], 0) for g in range(groups)]

    def other_half(i, m):
        return (0, 1 - m[4])

    def own_half(i, m):
        return (0, m[4])

    def build_rows(name, plan, jobs, after, cost=COST):
        sources = [source for job in jobs for source in job]
        return call(
            functools.partial(grad_rows_body, plan, len(jobs), count, groups), name, (1,),
            [pl.BlockSpec((group_tokens, extent), table_at) for _, table_at, _ in sources]
            + [pl.BlockSpec((group_tokens, large), data_at) for _, _, data_at in sources]
            + [glance] * len(after),
            [pl.BlockSpec((len(parts) * rows, large), lambda i, m: (0, 0)) for _, parts in plan],
            [jax.ShapeDtypeStruct((len(parts) * rows, large), BF16) for _, parts in plan],
            meta, (*[value for value, _, _ in sources] * 2, *after),
            scratch=[pltpu.VMEM((extent, group_tokens), F32)],
            room=room, cost=cost,
        )

    def beside(i, m):
        return (0, width // extent)

    jobs = [[(value, beside, at) for value in gathered] for at in (other_half, own_half)]
    if relay:
        collected = call(
            functools.partial(collect_body, planes), "collect", (1,),
            [pl.BlockSpec((tokens, extent), beside)] * planes
            + [pl.BlockSpec((tokens, large), other_half)] * planes
            + [pl.BlockSpec((tokens, large), own_half)] * planes
            + [glance],
            [pl.BlockSpec((planes * tokens, large + extent), lambda i, m: (0, 0))] * 2,
            [jax.ShapeDtypeStruct((planes * tokens, large + extent), BF16)] * 2,
            meta, (*gathered * 3, final_output),
            room=room,
        )
        near = [swap(value, 1 << number) for number, value in enumerate(collected)]
        made = build_rows("own_rows", ((0, (0, 1)), (1, (1,)), (2, (0,))), jobs, (collected[0],))
        arrived = [
            [(made[0], 0), (made[0], 1)], [None, (swap(made[1], 1), 0)], [(swap(made[2], 2), 0), None], [None, None],
        ]
    else:
        made = build_rows("own_rows", tuple((peer, (0, 1)) for peer in range(peers)), jobs, (final_output,))
        arrived = [[(made[0], 0), (made[0], 1)]]
        for peer in range(1, peers):
            got = swap(made[peer], peer)
            arrived.append([(got, 0), (got, 1)])

    padded = width + -(-3 * count // 128) * 128

    def combine(chosen, dtype, after):
        first, stride = chosen[0], len(chosen) > 1 and chosen[1] - chosen[0]
        columns = width if fold == 1 else large

        def part_of(k, i, m):
            return (lax.bitwise_xor(m[1], k * stride + first), jnp.minimum(i, width // columns - 1))

        blocks_of = [gathered[group] for group in chosen]
        return call(
            functools.partial(combine_body, peers, count, len(chosen)), f"combine{first}", (len(chosen), width // columns + 1),
            [pl.BlockSpec((group_tokens, extent), lambda k, i, m: (0, width // extent))] * len(chosen)
            + [pl.BlockSpec((group_tokens, columns), lambda k, i, m: (0, jnp.minimum(i, width // columns - 1)))] * len(chosen)
            + [glance]
            + [pl.BlockSpec((group_rows, columns), part_of)] * peers,
            pl.BlockSpec((group_tokens, columns), lambda k, i, m: (k, i)),
            jax.ShapeDtypeStruct((len(chosen) * group_tokens, padded), dtype),
            meta, (*blocks_of, *blocks_of, after, *returned),
            scratch=[
                pltpu.VMEM((extent, group_tokens), F32),
                pltpu.VMEM((2 * group_tokens, peers * group_rows), BF16),
                pltpu.VMEM((peers * group_rows, group_tokens), F32),
                pltpu.VMEM((peers, group_tokens), F32),
            ],
            room=room,
        )

    if fold == 1:
        leaving = combine(range(1, planes, 2), BF16, made[0])
        combine_done = combine(range(0, planes, 2), F32, leaving)
        sums = [combine_done[k * tokens : (k + 1) * tokens] for k in range(planes // 2)]
    else:
        parts = [combine([group], F32, made[0]) for group in range(groups)]
        combine_done = parts[-1]
        sums = [parts[k // fold][k % fold * tokens : (k % fold + 1) * tokens] for k in range(planes)]
        leaving = jnp.concatenate(sums[1::2], 0).astype(BF16)
        sums = sums[0::2]
    distance = 1
    first_sums = None
    while len(sums) > 1:
        got = swap(leaving, peers * distance)
        pieces = [got[k * tokens : (k + 1) * tokens].astype(F32) for k in range(len(sums))]
        sums = [mine + piece for mine, piece in zip(sums, pieces)]
        leaving = [value.astype(BF16) for value in sums[1::2]]
        leaving = leaving[0] if len(leaving) == 1 else jnp.concatenate(leaving, 0)
        sums = sums[0::2]
        first_sums = leaving if first_sums is None else first_sums
        distance *= 2
    summed = swap(leaving, peers * distance)

    if relay:
        near_jobs = [
            [(value, lambda i, m, k=k: (k, large // extent), lambda i, m, k=k: (k, 0)) for k in range(planes)]
            for value in near
        ]
        plan = ((0, (0,)), (2, (0,)), (0, (1,)), (1, (1,)))
        made = build_rows("near_rows", plan, near_jobs, (combine_done,), NEAR_COST)
        arrived[1][0], arrived[2][1] = (made[0], 0), (made[2], 0)
        arrived[3] = [(swap(made[1], 2), 0), (swap(made[3], 1), 0)]

    grads_shape = jax.ShapeDtypeStruct(blocks.shape, BF16)
    def rows_of(chosen):
        arrays, plan = [], []
        for peer in chosen:
            parts = []
            for value, at in arrived[peer]:
                known = [number for number, array in enumerate(arrays) if array is value]
                if not known:
                    arrays.append(value)
                parts.append((known[0] if known else len(arrays) - 1, at * rows))
            plan.append((peer, tuple(parts)))
        return arrays, tuple(plan)

    def inside_grad(chosen, earlier, after):
        arrays, plan = rows_of(chosen)
        operands = [matrix, *arrays, *after] + ([] if earlier is None else [earlier])
        return direct(
            functools.partial(inside_body, plan), f"inside{chosen[0]}",
            [grads_shape, jax.ShapeDtypeStruct((16, 128), F32)],
            meta, operands,
            out_specs=[anywhere, pl.BlockSpec(memory_space=pltpu.VMEM)],
            scratch=[
                pltpu.VMEM((len(chosen), block[0], block[2], inside), BF16),
                pltpu.SemaphoreType.DMA((len(chosen),)),
            ],
            aliases=None if earlier is None else {len(operands): 0},
            places={} if earlier is None else {len(operands) - 1: anywhere},
        )

    hidden_grads, token = inside_grad(range(last), None, (made[1][:16, :128], first_sums[:16, :128]))
    arrays, plan = rows_of(range(last))
    *totals_other, total_own = direct(
        functools.partial(weight_grad_body, plan, len(arrays), half), "weight_grad",
        [jax.ShapeDtypeStruct((inside, tile), BF16)] * half + [jax.ShapeDtypeStruct((inside, large), F32)],
        meta, (turned, *arrays, token),
    )
    totals_other = [exchange(value) for value in totals_other]
    last_other, last_own = arrived[last]
    rows_own = last_own[0] if relay else last_own[0][rows:]
    rows_other = last_other[0] if relay else last_other[0][:rows]
    followed = follow(rows_other, summed, last_own[0])
    rows_other = exchange(followed)

    combined, gate_grads = direct(
        functools.partial(finish_body, count), "finish",
        [jax.ShapeDtypeStruct((tokens, width), BF16), jax.ShapeDtypeStruct((top, tokens), F32)],
        meta, (ids_turned, sums[0], summed),
    )
    hidden_grads, _ = inside_grad([last], hidden_grads, (followed,))
    weight_grads = pl.pallas_call(
        functools.partial(last_body, half, None),
        name="last",
        out_shape=jax.ShapeDtypeStruct((inside, large), BF16),
        cost_estimate=pl.CostEstimate(flops=COST, bytes_accessed=COST, transcendentals=0),
        compiler_params=pltpu.CompilerParams(vmem_limit_bytes=room * VMEM_BYTES),
    )(turned_last, rows_own, turned_other, rows_other, total_own, *totals_other)

    if fold > 1:
        hidden_grads = hidden_grads.reshape(peers, planes, cap, inside).transpose(1, 0, 2, 3)
    return combined, gate_grads.T, hidden_grads.reshape(hidden.shape), weight_grads[None]


def solution(mesh):
    placed = (
        P(("expert", "dp"), None),
        P(("expert", "dp"), None),
        P("expert", "dp", None),
        P("expert", None, None),
        P(("expert", "dp"), None),
    )
    return jax.shard_map(
        per_device,
        mesh=mesh,
        in_specs=placed,
        out_specs=(
            P(("expert", "dp"), None),
            P(("expert", "dp"), None),
            P("expert", "dp", None),
            P("expert", None, "dp"),
        ),
        check_vma=False,
    )
```

profile of v0, /device:TPU:1, one launch (start us, length us, event | category | flops | bytes accessed | tf_op | source)
XLA Modules:
  0.0 136.9 jit_solution(3289625634198506223)
XLA Ops:
  1.3 6.7 %forward1.1 = (bf16[320,2048]{1,0:T(8,128)(2,1)}, bf16[320,2048]{1,0:T(8,128)(2,1)}) custom-call(s32[7]{0:T(128)} %stack.21.meta, bf16[4,4,80,768]{3,2,1,0:T(8,128)(2,1)} %bitcast.16, bf16[768,2048]{1,0:T(8,128)(2,1)} %bitcast.11), custom_call_target="tpu_custom_call" | custom-call | flops 1024 | bytes 1024 | tf_op jit(solution)/shard_map/forward1/pallas_call | solution.py:35
  8.0 2.1 %collective-permute-start.3 = (bf16[320,2048]{1,0:T(8,128)(2,1)}, bf16[320,2048]{1,0:T(8,128)(2,1)S(1)}, u32[]{:S(2)}, u32[]{:S(2)}) collective-permute-start(bf16[320,2048]{1,0:T(8,128)(2,1)} %get-tuple-element.27), channel_id=1, source_target_pairs={{0,2},{2,0},{4,6},{6,4},{8,10},{10,8},{12,14},{14,12},{16,18},{18,... | collective-permute-start | bytes 3932168 | tf_op jit(solution)/shard_map/ppermute | solution.py:309
  12.2 2.4 %collective-permute-start = (bf16[128,2176]{1,0:T(8,128)(2,1)S(1)}, bf16[128,2176]{1,0:T(8,128)(2,1)S(1)}, u32[]{:S(2)}, u32[]{:S(2)}) collective-permute-start(bf16[128,2176]{1,0:T(8,128)(2,1)S(1)} %pack.1.refs_3_.refs_0_.refs_4_.refs_8_.refs_12_.refs_2_), channel_id=1, source_target_pairs={{0,16},{2,18},{4,20},{6,22},{8,24},{10,26},{12,28},{14,30},{16,0},... | collective-permute-start | bytes 1671176 | tf_op jit(solution)/shard_map/ppermute | solution.py:309
  14.6 1.3 collective-permute-start.1
  15.9 1.5 %copy-done.1 = bf16[1,1280,768]{2,1,0:T(8,128)(2,1)S(1)} copy-done((bf16[1,1280,768]{2,1,0:T(8,128)(2,1)S(1)}, bf16[1,1280,768]{2,1,0:T(8,128)(2,1)}, u32[]{:S(2)}) %copy-start.1) | copy-done | bytes 1966104
  17.4 1.3 copy-done.2
  18.8 2.6 %forward3.1.refs_2_.refs_0_ = bf16[320,2048]{1,0:T(8,128)(2,1)S(1)} custom-call(s32[7]{0:T(128)S(1)} %copy-done.4, bf16[4,4,80,768]{3,2,1,0:T(8,128)(2,1)S(1)} %bitcast.17, bf16[768,2048]{1,0:T(8,128)(2,1)S(1)} %bitcast.12, bf16[320,2048]{1,0:T(8,128)(2,1)S(1)} %copy-done.2, bf16[128,2176]{1,0:T(8,128)(2,1)S(1)} %pack.1.refs_3_.refs_0_.refs_4_.refs_8_.refs_12_.refs_2_), custom_call_target="tpu_custom_call" | custom-call | flops 1024 | bytes 1024 | tf_op jit(solution)/shard_map/forward3/pallas_call | solution.py:18
  21.4 2.6 %forward0.1.after.refs_5_ = bf16[320,2048]{1,0:T(8,128)(2,1)S(1)} custom-call(s32[7]{0:T(128)S(1)} %copy-done.4, bf16[4,4,80,768]{3,2,1,0:T(8,128)(2,1)S(1)} %bitcast.18, bf16[768,2048]{1,0:T(8,128)(2,1)S(1)} %bitcast.13, bf16[320,2048]{1,0:T(8,128)(2,1)S(1)} %forward3.1.refs_2_.refs_0_, ...), custom_call_target="tpu_custom_call" | custom-call | flops 1024 | bytes 1024 | tf_op jit(solution)/shard_map/forward0/pallas_call | solution.py:18
  24.1 1.7 %turn.1 = (bf16[4,768,320]{2,1,0:T(8,128)(2,1)S(1)}, bf16[320,768]{1,0:T(8,128)(2,1)S(1)}, bf16[768,320]{1,0:T(8,128)(2,1)S(1)}) custom-call(s32[7]{0:T(128)S(1)} %copy-done.4, bf16[4,4,80,768]{3,2,1,0:T(8,128)(2,1)S(1)} %bitcast.19, bf16[320,2048]{1,0:T(8,128)(2,1)S(1)} %forward0.1.after.refs_5_), custom_call_target="tpu_custom_call" | custom-call | flops 1024 | bytes 1024 | tf_op jit(solution)/shard_map/turn/pallas_call | solution.py:18
  25.7 1.9 %collective-permute-start.4 = (bf16[320,768]{1,0:T(8,128)(2,1)S(1)}, bf16[320,768]{1,0:T(8,128)(2,1)S(1)}, u32[]{:S(2)}, u32[]{:S(2)}) collective-permute-start(bf16[320,768]{1,0:T(8,128)(2,1)S(1)} %get-tuple-element.28), channel_id=1, source_target_pairs={{0,1},{1,0},{2,3},{3,2},{4,5},{5,4},{6,7},{7,6},{8,9},{9,8},{10,11... | collective-permute-start | bytes 1474568 | tf_op jit(solution)/shard_map/ppermute | solution.py:312
  27.6 1.5 %collective-permute-done.4.hidden = bf16[320,768]{1,0:T(8,128)(2,1)S(1)} collective-permute-done((bf16[320,768]{1,0:T(8,128)(2,1)S(1)}, bf16[320,768]{1,0:T(8,128)(2,1)S(1)}, u32[]{:S(2)}, u32[]{:S(2)}) %collective-permute-start.4) | collective-permute-done | bytes 491552 | tf_op jit(solution)/shard_map/ppermute | solution.py:312
  29.8 8.8 %collective-permute-done.refs_5_.refs_2_.refs_6_.refs_10_.refs_14_.refs_1_.refs_3_ = bf16[128,2176]{1,0:T(8,128)(2,1)S(1)} collective-permute-done((bf16[128,2176]{1,0:T(8,128)(2,1)S(1)}, bf16[128,2176]{1,0:T(8,128)(2,1)S(1)}, u32[]{:S(2)}, u32[]{:S(2)}) %collective-permute-start) | collective-permute-done | bytes 557088 | tf_op jit(solution)/shard_map/ppermute | solution.py:309
  39.7 1.3 collective-permute-start.5
  41.0 1.3 collective-permute-start.6
  42.2 9.7 %collective-permute-done.5.refs_3_.refs_7_.refs_11_.refs_15_.refs_1_ = bf16[128,2176]{1,0:T(8,128)(2,1)S(1)} collective-permute-done((bf16[128,2176]{1,0:T(8,128)(2,1)S(1)}, bf16[128,2176]{1,0:T(8,128)(2,1)S(1)}, u32[]{:S(2)}, u32[]{:S(2)}) %collective-permute-start.5) | collective-permute-done | bytes 557088 | tf_op jit(solution)/shard_map/ppermute | solution.py:309
  53.0 1.3 collective-permute-start.10
  54.7 2.1 %own_rows.1 = (bf16[640,1024]{1,0:T(8,128)(2,1)S(1)}, bf16[320,1024]{1,0:T(8,128)(2,1)S(1)}, bf16[320,1024]{1,0:T(8,128)(2,1)S(1)}) custom-call(s32[7]{0:T(128)S(1)} %copy-done.4, bf16[128,2176]{1,0:T(8,128)(2,1)S(1)} %pack.1.refs_3_.refs_0_.refs_4_.refs_8_.refs_12_.refs_2_, ...), custom_call_target="tpu_custom_call" | custom-call | flops 1024 | bytes 1024 | tf_op jit(solution)/shard_map/own_rows/pallas_call | solution.py:18
  56.8 13.2 %collective-permute-done.6.refs_8_ = bf16[320,2048]{1,0:T(8,128)(2,1)S(1)} collective-permute-done((bf16[320,2048]{1,0:T(8,128)(2,1)S(1)}, bf16[320,2048]{1,0:T(8,128)(2,1)S(1)}, u32[]{:S(2)}, u32[]{:S(2)}) %collective-permute-start.6) | collective-permute-done | bytes 1310752 | tf_op jit(solution)/shard_map/ppermute | solution.py:309
  70.0 4.1 %combine1.1.refs_4_ = bf16[256,2176]{1,0:T(8,128)(2,1)S(1)} custom-call(s32[7]{0:T(128)S(1)} %copy-done.4, bf16[128,2176]{1,0:T(8,128)(2,1)S(1)} %collective-permute-done.1.refs_4_.refs_1_.refs_5_.refs_9_.refs_13_.refs_0_.refs_2_, bf16[128,2176]{1,0:T(8,128)(2,1)S(1)} %collective-permute-done.5.refs_3_.refs_7_.refs_11_.refs_15_.refs_1_, ...), custom_call_target="tpu_custom_call" | custom-call | flops 1024 | bytes 1024 | tf_op jit(solution)/shard_map/combine1/pallas_call | solution.py:18
  76.0 4.0 %combine0.1.refs_16_ = f32[256,2176]{1,0:T(8,128)S(1)} custom-call(s32[7]{0:T(128)S(1)} %copy-done.4, bf16[128,2176]{1,0:T(8,128)(2,1)S(1)} %pack.1.refs_3_.refs_0_.refs_4_.refs_8_.refs_12_.refs_2_, bf16[128,2176]{1,0:T(8,128)(2,1)S(1)} %collective-permute-done.refs_5_.refs_2_.refs_6_.refs_10_.refs_14_.refs_1_.refs_3_, ...), custom_call_target="tpu_custom_call" | custom-call | flops 1024 | bytes 1024 | tf_op jit(solution)/shard_map/combine0/pallas_call | solution.py:18
  80.1 17.8 %collective-permute-done.10.refs_4_.refs_5_.refs_6_.refs_7_.refs_12_.refs_13_.refs_14_.refs_15_ = bf16[512,1152]{1,0:T(8,128)(2,1)S(1)} collective-permute-done((bf16[512,1152]{1,0:T(8,128)(2,1)S(1)}, bf16[512,1152]{1,0:T(8,128)(2,1)S(1)}, u32[]{:S(2)}, u32[]{:S(2)}) %collective-permute-start.10) | collective-permute-done | bytes 1179680 | tf_op jit(solution)/shard_map/ppermute | solution.py:309
  97.8 1.7 %near_rows.1 = (bf16[320,1024]{1,0:T(8,128)(2,1)S(1)}, bf16[320,1024]{1,0:T(8,128)(2,1)S(1)}, bf16[320,1024]{1,0:T(8,128)(2,1)S(1)}, bf16[320,1024]{1,0:T(8,128)(2,1)S(1)}) custom-call(s32[7]{0:T(128)S(1)} %copy-done.4, bf16[512,1152]{1,0:T(8,128)(2,1)S(1)} %collective-permute-done.9.refs_0_.refs_1_.refs_2_.refs_3_.refs_8_.refs_9_.refs_10_.refs_11_, ...), custom_call_target="tpu_custom_call" | custom-call | flops 10000000000 | bytes 1024 | tf_op jit(solution)/shard_map/near_rows/pallas_call | solution.py:18
  101.4 2.4 %collective-permute-start.8 = (bf16[128,2176]{1,0:T(8,128)(2,1)S(1)}, bf16[128,2176]{1,0:T(8,128)(2,1)S(1)}, u32[]{:S(2)}, u32[]{:S(2)}) collective-permute-start(bf16[128,2176]{1,0:T(8,128)(2,1)S(1)} %get-tuple-element.48), channel_id=1, source_target_pairs={{0,16},{2,18},{4,20},{6,22},{8,24},{10,26},{12,28},{14,30},{16,0},... | collective-permute-start | bytes 1671176 | tf_op jit(solution)/shard_map/ppermute | solution.py:309
  103.7 5.7 %collective-permute-done.13.refs_2_ = bf16[320,1024]{1,0:T(8,128)(2,1)S(1)} collective-permute-done((bf16[320,1024]{1,0:T(8,128)(2,1)S(1)}, bf16[320,1024]{1,0:T(8,128)(2,1)S(1)}, u32[]{:S(2)}, u32[]{:S(2)}) %collective-permute-start.13) | collective-permute-done | bytes 655392 | tf_op jit(solution)/shard_map/ppermute | solution.py:309
  109.4 2.5 %collective-permute-done.14.refs_3_ = bf16[320,1024]{1,0:T(8,128)(2,1)S(1)} collective-permute-done((bf16[320,1024]{1,0:T(8,128)(2,1)S(1)}, bf16[320,1024]{1,0:T(8,128)(2,1)S(1)}, u32[]{:S(2)}, u32[]{:S(2)}) %collective-permute-start.14) | collective-permute-done | bytes 655392 | tf_op jit(solution)/shard_map/ppermute | solution.py:309
  111.9 4.7 %inside0.1 = (bf16[4,4,80,768]{3,2,1,0:T(8,128)(2,1)}, f32[16,128]{1,0:T(8,128)S(1)}) custom-call(s32[7]{0:T(128)S(1)} %copy-done.4, bf16[768,2048]{1,0:T(8,128)(2,1)S(1)} %bitcast.14, bf16[640,1024]{1,0:T(8,128)(2,1)S(1)} %get-tuple-element.30.refs_4_.refs_0_, bf16[320,1024]{1,0:T(8,128)(2,1)S(1)} %get-tuple-element.36.refs_1_, ...), custom_call_target="tpu_custom_call" | custom-call | flops 1024 | bytes 1024 | tf_op jit(solution)/shard_map/inside0/pallas_call | solution.py:35
  116.6 5.6 %weight_grad.1 = (bf16[768,512]{1,0:T(8,128)(2,1)S(1)}, bf16[768,512]{1,0:T(8,128)(2,1)S(1)}, f32[768,1024]{1,0:T(8,128)S(1)}) custom-call(s32[7]{0:T(128)S(1)} %copy-done.4, bf16[4,768,320]{2,1,0:T(8,128)(2,1)S(1)} %get-tuple-element.43.turned, bf16[640,1024]{1,0:T(8,128)(2,1)S(1)} %get-tuple-element.30.refs_4_.refs_0_, ...), custom_call_target="tpu_custom_call" | custom-call | flops 1024 | bytes 1024 | tf_op jit(solution)/shard_map/weight_grad/pallas_call | solution.py:35
  122.1 3.3 %collective-permute-start.16 = (bf16[768,512]{1,0:T(8,128)(2,1)S(1)}, bf16[768,512]{1,0:T(8,128)(2,1)S(1)}, u32[]{:S(2)}, u32[]{:S(2)}) collective-permute-start(bf16[768,512]{1,0:T(8,128)(2,1)S(1)} %get-tuple-element.46), channel_id=1, source_target_pairs={{0,1},{1,0},{2,3},{3,2},{4,5},{5,4},{6,7},{7,6},{8,9},{9,8},{10,11... | collective-permute-start | bytes 2359304 | tf_op jit(solution)/shard_map/ppermute | solution.py:312
  126.0 2.7 %collective-permute-done.8.arrived.refs_1_ = bf16[128,2176]{1,0:T(8,128)(2,1)S(1)} collective-permute-done((bf16[128,2176]{1,0:T(8,128)(2,1)S(1)}, bf16[128,2176]{1,0:T(8,128)(2,1)S(1)}, u32[]{:S(2)}, u32[]{:S(2)}) %collective-permute-start.8) | collective-permute-done | bytes 557088 | tf_op jit(solution)/shard_map/ppermute | solution.py:309
  129.2 1.6 %finish.1 = (bf16[128,2048]{1,0:T(8,128)(2,1)}, f32[8,128]{1,0:T(8,128)}) custom-call(s32[7]{0:T(128)S(1)} %copy-done.4, s32[8,128]{1,0:T(8,128)S(1)} %bitcast.21, f32[128,2176]{1,0:T(8,128)S(1)} %get-tuple-element.49.kept, bf16[128,2176]{1,0:T(8,128)(2,1)S(1)} %collective-permute-done.8.arrived.refs_1_), custom_call_target="tpu_custom_call" | custom-call | flops 1024 | bytes 1024 | tf_op jit(solution)/shard_map/finish/pallas_call | solution.py:35
  130.8 3.1 %inside3.1 = (bf16[4,4,80,768]{3,2,1,0:T(8,128)(2,1)}, f32[16,128]{1,0:T(8,128)}) custom-call(s32[7]{0:T(128)S(1)} %copy-done.4, bf16[768,2048]{1,0:T(8,128)(2,1)S(1)} %bitcast.15, bf16[320,1024]{1,0:T(8,128)(2,1)S(1)} %collective-permute-done.11.refs_0_, ...), custom_call_target="tpu_custom_call", output_to_operand_aliasing={{0}: (5, {})} | custom-call | flops 1024 | bytes 1024 | tf_op jit(solution)/shard_map/inside3/pallas_call | solution.py:35
  133.9 3.0 %last.1 = bf16[768,1024]{1,0:T(8,128)(2,1)} custom-call(bf16[768,320]{1,0:T(8,128)(2,1)S(1)} %get-tuple-element.42.turned, bf16[320,1024]{1,0:T(8,128)(2,1)S(1)} %collective-permute-done.12.refs_2_.refs_1_.rows, bf16[768,320]{1,0:T(8,128)(2,1)S(1)} %turn_other.1.refs_3_.turned_other, bf16[320,1024]{1,0:T(8,128)(2,1)S(1)} %collective-permute-done.15.rows_other, ...), custom_call_target="tpu_custom_call" | custom-call | flops 1024 | bytes 1024 | tf_op jit(solution)/shard_map/last/pallas_call | solution.py:559
  (43 shorter events, 10.7 us)
Async XLA Ops:
  1.3 10.1 %copy-start.3 = (bf16[128,2048]{1,0:T(8,128)(2,1)S(1)}, bf16[128,2048]{1,0:T(8,128)(2,1)}, u32[]{:S(2)}) copy-start(bf16[128,2048]{1,0:T(8,128)(2,1)} %grad.1) | copy-start | bytes 1572868
  1.3 10.1 %copy-start.4 = (s32[7]{0:T(128)S(1)}, s32[7]{0:T(128)}, u32[]{:S(2)}) copy-start(s32[7]{0:T(128)} %stack.21.meta) | copy-start | bytes 88
  1.3 10.1 %copy-start.5 = (s32[128,8]{0,1:T(8,128)S(1)}, s32[128,8]{0,1:T(8,128)}, u32[]{:S(2)}) copy-start(s32[128,8]{0,1:T(8,128)} %param.5) | copy-start | bytes 12292
  1.3 10.1 %copy-start.6 = (f32[128,8]{0,1:T(8,128)S(1)}, f32[128,8]{0,1:T(8,128)}, u32[]{:S(2)}) copy-start(f32[128,8]{0,1:T(8,128)} %param.6) | copy-start | bytes 12292
  1.3 14.6 %copy-start = (bf16[1,768,2048]{2,1,0:T(8,128)(2,1)S(1)}, bf16[1,768,2048]{2,1,0:T(8,128)(2,1)}, u32[]{:S(2)}) copy-start(bf16[1,768,2048]{2,1,0:T(8,128)(2,1)} %param.8) | copy-start | bytes 9437188
  8.0 30.8 %collective-permute-start.3 = (bf16[320,2048]{1,0:T(8,128)(2,1)}, bf16[320,2048]{1,0:T(8,128)(2,1)S(1)}, u32[]{:S(2)}, u32[]{:S(2)}) collective-permute-start(bf16[320,2048]{1,0:T(8,128)(2,1)} %get-tuple-element.27), channel_id=1, source_target_pairs={{0,2},{2,0},{4,6},{6,4},{8,10},{10,8},{12,14},{14,12},{16,18},{18,... | collective-permute-start | bytes 3932168 | tf_op jit(solution)/shard_map/ppermute | solution.py:309
  10.1 29.5 %collective-permute-start.2 = (bf16[320,2048]{1,0:T(8,128)(2,1)}, bf16[320,2048]{1,0:T(8,128)(2,1)S(1)}, u32[]{:S(2)}, u32[]{:S(2)}) collective-permute-start(bf16[320,2048]{1,0:T(8,128)(2,1)} %get-tuple-element.26.refs_2_), channel_id=1, source_target_pairs={{0,4},{2,6},{4,0},{6,2},{8,12},{10,14},{12,8},{14,10},{16,20},{18,... | collective-permute-start | bytes 3932168 | tf_op jit(solution)/shard_map/ppermute | solution.py:309
  12.2 26.4 %collective-permute-start = (bf16[128,2176]{1,0:T(8,128)(2,1)S(1)}, bf16[128,2176]{1,0:T(8,128)(2,1)S(1)}, u32[]{:S(2)}, u32[]{:S(2)}) collective-permute-start(bf16[128,2176]{1,0:T(8,128)(2,1)S(1)} %pack.1.refs_3_.refs_0_.refs_4_.refs_8_.refs_12_.refs_2_), channel_id=1, source_target_pairs={{0,16},{2,18},{4,20},{6,22},{8,24},{10,26},{12,28},{14,30},{16,0},... | collective-permute-start | bytes 1671176 | tf_op jit(solution)/shard_map/ppermute | solution.py:309
  14.6 24.1 %collective-permute-start.1 = (bf16[128,2176]{1,0:T(8,128)(2,1)S(1)}, bf16[128,2176]{1,0:T(8,128)(2,1)S(1)}, u32[]{:S(2)}, u32[]{:S(2)}) collective-permute-start(bf16[128,2176]{1,0:T(8,128)(2,1)S(1)} %pack.1.refs_3_.refs_0_.refs_4_.refs_8_.refs_12_.refs_2_), channel_id=1, source_target_pairs={{0,8},{2,10},{4,12},{6,14},{8,0},{10,2},{12,4},{14,6},{16,24},{18,... | collective-permute-start | bytes 1671176 | tf_op jit(solution)/shard_map/ppermute | solution.py:309
  15.9 1.5 %copy-start.1 = (bf16[1,1280,768]{2,1,0:T(8,128)(2,1)S(1)}, bf16[1,1280,768]{2,1,0:T(8,128)(2,1)}, u32[]{:S(2)}) copy-start(bf16[1,1280,768]{2,1,0:T(8,128)(2,1)} %param.7) | copy-start | bytes 5898244
  17.4 1.3 copy-start.2
  25.7 3.3 %collective-permute-start.4 = (bf16[320,768]{1,0:T(8,128)(2,1)S(1)}, bf16[320,768]{1,0:T(8,128)(2,1)S(1)}, u32[]{:S(2)}, u32[]{:S(2)}) collective-permute-start(bf16[320,768]{1,0:T(8,128)(2,1)S(1)} %get-tuple-element.28), channel_id=1, source_target_pairs={{0,1},{1,0},{2,3},{3,2},{4,5},{5,4},{6,7},{7,6},{8,9},{9,8},{10,11... | collective-permute-start | bytes 1474568 | tf_op jit(solution)/shard_map/ppermute | solution.py:312
  39.7 12.3 %collective-permute-start.5 = (bf16[128,2176]{1,0:T(8,128)(2,1)S(1)}, bf16[128,2176]{1,0:T(8,128)(2,1)S(1)}, u32[]{:S(2)}, u32[]{:S(2)}) collective-permute-start(bf16[128,2176]{1,0:T(8,128)(2,1)S(1)} %follow.4), channel_id=1, source_target_pairs={{0,8},{2,10},{4,12},{6,14},{8,0},{10,2},{12,4},{14,6},{16,24},{18,... | collective-permute-start | bytes 1671176 | tf_op jit(solution)/shard_map/ppermute | solution.py:309
  41.0 29.1 %collective-permute-start.6 = (bf16[320,2048]{1,0:T(8,128)(2,1)S(1)}, bf16[320,2048]{1,0:T(8,128)(2,1)S(1)}, u32[]{:S(2)}, u32[]{:S(2)}) collective-permute-start(bf16[320,2048]{1,0:T(8,128)(2,1)S(1)} %follow.3.refs_1_.refs_12_), channel_id=1, source_target_pairs={{0,6},{2,4},{4,2},{6,0},{8,14},{10,12},{12,10},{14,8},{16,22},{18,... | collective-permute-start | bytes 3932168 | tf_op jit(solution)/shard_map/ppermute | solution.py:309
  53.0 44.8 %collective-permute-start.10 = (bf16[512,1152]{1,0:T(8,128)(2,1)S(1)}, bf16[512,1152]{1,0:T(8,128)(2,1)S(1)}, u32[]{:S(2)}, u32[]{:S(2)}) collective-permute-start(bf16[512,1152]{1,0:T(8,128)(2,1)S(1)} %get-tuple-element.33), channel_id=1, source_target_pairs={{0,4},{2,6},{4,0},{6,2},{8,12},{10,14},{12,8},{14,10},{16,20},{18,... | collective-permute-start | bytes 3538952 | tf_op jit(solution)/shard_map/ppermute | solution.py:309
  54.3 43.5 %collective-permute-start.9 = (bf16[512,1152]{1,0:T(8,128)(2,1)S(1)}, bf16[512,1152]{1,0:T(8,128)(2,1)S(1)}, u32[]{:S(2)}, u32[]{:S(2)}) collective-permute-start(bf16[512,1152]{1,0:T(8,128)(2,1)S(1)} %get-tuple-element.29.refs_16_), channel_id=1, source_target_pairs={{0,2},{2,0},{4,6},{6,4},{8,10},{10,8},{12,14},{14,12},{16,18},{18,... | collective-permute-start | bytes 3538952 | tf_op jit(solution)/shard_map/ppermute | solution.py:309
  74.2 27.0 %collective-permute-start.7 = (bf16[256,2176]{1,0:T(8,128)(2,1)S(1)}, bf16[256,2176]{1,0:T(8,128)(2,1)S(1)}, u32[]{:S(2)}, u32[]{:S(2)}) collective-permute-start(bf16[256,2176]{1,0:T(8,128)(2,1)S(1)} %combine1.1.refs_4_), channel_id=1, source_target_pairs={{0,8},{2,10},{4,12},{6,14},{8,0},{10,2},{12,4},{14,6},{16,24},{18,... | collective-permute-start | bytes 3342344 | tf_op jit(solution)/shard_map/ppermute | solution.py:309
  74.4 35.0 %collective-permute-start.13 = (bf16[320,1024]{1,0:T(8,128)(2,1)S(1)}, bf16[320,1024]{1,0:T(8,128)(2,1)S(1)}, u32[]{:S(2)}, u32[]{:S(2)}) collective-permute-start(bf16[320,1024]{1,0:T(8,128)(2,1)S(1)} %get-tuple-element.37), channel_id=1, source_target_pairs={{0,2},{2,0},{4,6},{6,4},{8,10},{10,8},{12,14},{14,12},{16,18},{18,... | collective-permute-start | bytes 1966088 | tf_op jit(solution)/shard_map/ppermute | solution.py:309
  75.1 36.8 %collective-permute-start.14 = (bf16[320,1024]{1,0:T(8,128)(2,1)S(1)}, bf16[320,1024]{1,0:T(8,128)(2,1)S(1)}, u32[]{:S(2)}, u32[]{:S(2)}) collective-permute-start(bf16[320,1024]{1,0:T(8,128)(2,1)S(1)} %get-tuple-element.38), channel_id=1, source_target_pairs={{0,4},{2,6},{4,0},{6,2},{8,12},{10,14},{12,8},{14,10},{16,20},{18,... | collective-permute-start | bytes 1966088 | tf_op jit(solution)/shard_map/ppermute | solution.py:309
  99.5 26.4 %collective-permute-start.12 = (bf16[320,1024]{1,0:T(8,128)(2,1)S(1)}, bf16[320,1024]{1,0:T(8,128)(2,1)S(1)}, u32[]{:S(2)}, u32[]{:S(2)}) collective-permute-start(bf16[320,1024]{1,0:T(8,128)(2,1)S(1)} %get-tuple-element.35), channel_id=1, source_target_pairs={{0,2},{2,0},{4,6},{6,4},{8,10},{10,8},{12,14},{14,12},{16,18},{18,... | collective-permute-start | bytes 1966088 | tf_op jit(solution)/shard_map/ppermute | solution.py:309
  99.9 26.0 %collective-permute-start.11 = (bf16[320,1024]{1,0:T(8,128)(2,1)S(1)}, bf16[320,1024]{1,0:T(8,128)(2,1)S(1)}, u32[]{:S(2)}, u32[]{:S(2)}) collective-permute-start(bf16[320,1024]{1,0:T(8,128)(2,1)S(1)} %get-tuple-element.34), channel_id=1, source_target_pairs={{0,4},{2,6},{4,0},{6,2},{8,12},{10,14},{12,8},{14,10},{16,20},{18,... | collective-permute-start | bytes 1966088 | tf_op jit(solution)/shard_map/ppermute | solution.py:309
  101.4 27.3 %collective-permute-start.8 = (bf16[128,2176]{1,0:T(8,128)(2,1)S(1)}, bf16[128,2176]{1,0:T(8,128)(2,1)S(1)}, u32[]{:S(2)}, u32[]{:S(2)}) collective-permute-start(bf16[128,2176]{1,0:T(8,128)(2,1)S(1)} %get-tuple-element.48), channel_id=1, source_target_pairs={{0,16},{2,18},{4,20},{6,22},{8,24},{10,26},{12,28},{14,30},{16,0},... | collective-permute-start | bytes 1671176 | tf_op jit(solution)/shard_map/ppermute | solution.py:309
  122.1 11.8 %collective-permute-start.16 = (bf16[768,512]{1,0:T(8,128)(2,1)S(1)}, bf16[768,512]{1,0:T(8,128)(2,1)S(1)}, u32[]{:S(2)}, u32[]{:S(2)}) collective-permute-start(bf16[768,512]{1,0:T(8,128)(2,1)S(1)} %get-tuple-element.46), channel_id=1, source_target_pairs={{0,1},{1,0},{2,3},{3,2},{4,5},{5,4},{6,7},{7,6},{8,9},{9,8},{10,11... | collective-permute-start | bytes 2359304 | tf_op jit(solution)/shard_map/ppermute | solution.py:312
  125.5 8.5 %collective-permute-start.17 = (bf16[768,512]{1,0:T(8,128)(2,1)S(1)}, bf16[768,512]{1,0:T(8,128)(2,1)S(1)}, u32[]{:S(2)}, u32[]{:S(2)}) collective-permute-start(bf16[768,512]{1,0:T(8,128)(2,1)S(1)} %get-tuple-element.47), channel_id=1, source_target_pairs={{0,1},{1,0},{2,3},{3,2},{4,5},{5,4},{6,7},{7,6},{8,9},{9,8},{10,11... | collective-permute-start | bytes 2359304 | tf_op jit(solution)/shard_map/ppermute | solution.py:312
  128.7 5.2 %collective-permute-start.15 = (bf16[320,1024]{1,0:T(8,128)(2,1)S(1)}, bf16[320,1024]{1,0:T(8,128)(2,1)S(1)}, u32[]{:S(2)}, u32[]{:S(2)}) collective-permute-start(bf16[320,1024]{1,0:T(8,128)(2,1)S(1)} %follow.5.refs_2_), channel_id=1, source_target_pairs={{0,1},{1,0},{2,3},{3,2},{4,5},{5,4},{6,7},{7,6},{8,9},{9,8},{10,11... | collective-permute-start | bytes 1966088 | tf_op jit(solution)/shard_map/ppermute | solution.py:312
where the time goes:
time: 137 us
  waiting for transfers between devices  63.2 us (46%)
  Pallas kernels  46.2 us (34%)
  starting transfers between devices  22.9 us (17%)
  local copies, waits for them, and re-layouts  3.6 us (3%)
    ppermute x14, waiting for transfers between devices, swap(): lax.ppermute(value, 'expert', [(e, e ^ distance) for e in range(count)])  61.7 us
    pallas_call x5, Pallas kernels, direct(): pl.pallas_call(body, name=name, in_specs=[smem] + [places.get(at, vmem) f...  21.7 us
    pallas_call x10, Pallas kernels, call(): pl.pallas_call(body, name=name, grid_spec=pltpu.PrefetchScalarGridSpec(nu...  21.6 us
    ppermute x14, starting transfers between devices, swap(): lax.ppermute(value, 'expert', [(e, e ^ distance) for e in range(count)])  17.2 us
    ppermute x4, starting transfers between devices, exchange(): return lax.ppermute(value, 'dp', [(0, 1), (1, 0)])  5.75 us
    pallas_call x1, Pallas kernels, per_device(): pl.pallas_call(functools.partial(last_body, half, None), name='last', out...  2.99 us
    unnamed x16, local copies, waits for them, and re-layouts  2.97 us
  transfers between devices with their start and end apart: 18, of which 11 were waited for; matrix products, arithmetic and copies ran while one was open for 0% of the time, Pallas kernels for 27%

commit v1 on v0

--- a/solution.py
+++ b/solution.py
@@ -28,7 +28,7 @@
     )(scalars, *operands)
 
 
-def direct(body, name, out_shape, scalars, operands, out_specs=None, scratch=(), aliases=None, places=None, room=1):
+def direct(body, name, out_shape, scalars, operands, out_specs=None, scratch=(), aliases=None, places=None, room=1, cost=COST):
     places = places or {}
     vmem, smem = pl.BlockSpec(memory_space=pltpu.VMEM), pl.BlockSpec(memory_space=pltpu.SMEM)
     several = isinstance(out_shape, (list, tuple))
@@ -40,7 +40,7 @@
         out_shape=out_shape,
         scratch_shapes=scratch,
         input_output_aliases=aliases or {},
-        cost_estimate=pl.CostEstimate(flops=COST, bytes_accessed=COST, transcendentals=0),
+        cost_estimate=pl.CostEstimate(flops=cost, bytes_accessed=COST, transcendentals=0),
         compiler_params=pltpu.CompilerParams(vmem_limit_bytes=int(room * VMEM_BYTES)),
     )(scalars, *operands)
 
@@ -91,13 +91,15 @@
 
 
 def collect_body(number, meta, *refs):
-    tables, sides, outs = refs[:number], (refs[number : 2 * number], refs[2 * number : 3 * number]), refs[-2:]
-    tokens = tables[0].shape[0]
-    for side, out in zip(sides, outs):
-        large = side[0].shape[1]
+    blocks, outs = refs[:number], refs[-2:]
+    tokens = blocks[0].shape[0]
+    extent = 2 * outs[0].shape[1] - blocks[0].shape[1]
+    large = outs[0].shape[1] - extent
+    for half, out in enumerate(outs):
+        start = pl.multiple_of(lax.bitwise_xor(1 - meta[4], half) * large, large)
         for k in range(number):
-            out[k * tokens : (k + 1) * tokens, :large] = side[k][...]
-            out[k * tokens : (k + 1) * tokens, large:] = tables[k][...]
+            out[k * tokens : (k + 1) * tokens, :large] = blocks[k][:, pl.ds(start, large)]
+            out[k * tokens : (k + 1) * tokens, large:] = blocks[k][:, 2 * large :]
 
 
 def forward_body(meta, hidden, weight, out):
@@ -168,6 +170,71 @@
                 out[pl.ds(place + part * groups * rows, rows), :] = value[at * rows : (at + 1) * rows]
 
 
+def direct_rows_body(plan, jobs, number, count, meta, *refs):
+    arrays, outs, table = refs[:number], refs[-1 - len(plan) : -1], refs[-1]
+    extent, tokens = table.shape
+    large = outs[0].shape[1]
+    rows = outs[0].shape[0] // len(plan[0][1]) // len(jobs[0])
+    for job, sources in enumerate(jobs):
+        asked = [(out, peer, parts.index(job)) for out, (peer, parts) in zip(outs, plan) if job in parts]
+        for group, (operand, first, whole) in enumerate(sources):
+            here = slice(first, first + tokens)
+            wide = 2 * large if whole else large
+            table[...] = arrays[operand][here, wide : wide + extent].astype(F32).T
+            choices, row_gates = [], []
+            for _, peer, _ in asked:
+                match, gate = selection(table, count, lax.bitwise_xor(meta[3], peer), rows)
+                choices.append(jnp.where(match, 1.0, 0.0))
+                row_gates.append(jnp.sum(jnp.where(match, gate, 0.0), 1, keepdims=True))
+            if whole:
+                columns = pl.ds(pl.multiple_of(lax.bitwise_xor(1 - meta[4], job) * large, large), large)
+            else:
+                columns = slice(0, large)
+            choice = jnp.concatenate(choices, 0).astype(BF16)
+            picked = jnp.dot(choice, arrays[operand][here, columns], preferred_element_type=F32)
+            value = (picked * jnp.concatenate(row_gates, 0)).astype(BF16)
+            place = pl.multiple_of(lax.bitwise_xor(meta[1], group) * rows, rows)
+            for at, (out, _, part) in enumerate(asked):
+                out[pl.ds(place + part * len(sources) * rows, rows), :] = value[at * rows : (at + 1) * rows]
+
+
+def direct_combine_body(peers, count, cap, chosen, meta, *refs):
+    blocks, returned, (part, table) = refs[: len(chosen)], refs[len(chosen) + 1 : -2], refs[-2:]
+    extent, length = table.shape
+    width = returned[0].shape[1]
+    chunk = min(512, width)
+    for number, k in enumerate(chosen):
+        here = slice(number * length, (number + 1) * length)
+        table[...] = blocks[number][:, width:].astype(F32).T
+        start = pl.multiple_of(lax.bitwise_xor(meta[1], k) * cap, cap)
+        highs, lows, marks = [], [], []
+        for peer in range(peers):
+            match, gate = selection(table, count, lax.bitwise_xor(meta[3], peer), cap)
+            high = gate.astype(BF16).astype(F32)
+            marks.append(jnp.where(match, 1.0, 0.0))
+            highs.append(jnp.where(match, high, 0.0))
+            lows.append(jnp.where(match, gate - high, 0.0))
+        weights = jnp.concatenate([jnp.concatenate(highs, 0).T, jnp.concatenate(lows, 0).T], 0).astype(BF16)
+        products = jnp.zeros((peers * cap, length), F32)
+        for at in range(0, width, chunk):
+            columns = slice(at, at + chunk)
+            value = jnp.concatenate([ref[pl.ds(start, cap), columns] for ref in returned], 0)
+            total = jnp.dot(weights, value, preferred_element_type=F32)
+            part[here, columns] = (total[:length] + total[length:]).astype(part.dtype)
+            products = products + lax.dot_general(
+                value, blocks[number][:, columns], (((1,), (1,)), ((), ())), preferred_element_type=F32
+            )
+        products = products * jnp.concatenate(marks, 0)
+        inner = [jnp.sum(products[peer * cap : (peer + 1) * cap], 0, keepdims=True) for peer in range(peers)]
+        beside = part.shape[1] - width
+        row = lax.broadcasted_iota(jnp.int32, (beside, length), 0)
+        placed = jnp.zeros((beside, length), F32)
+        for peer in range(peers):
+            for at, piece in enumerate(pieces_of(inner[peer])):
+                placed = jnp.where(row == at * count + lax.bitwise_xor(meta[3], peer), piece, placed)
+        part[here, width:] = placed.T.astype(part.dtype)
+
+
 def combine_body(peers, count, number, meta, *refs):
     packed, tokens, returned = refs[:number], refs[number : 2 * number], refs[2 * number + 1 : 2 * number + 1 + peers]
     part, table, weights, marks, inner = refs[-5:]
@@ -257,16 +324,21 @@
 
 
 def last_body(half, meta, turned, rows, turned_other, rows_other, earlier, *refs):
-    others, grads = refs[:half], refs[-1]
+    others, (grads, store, sems) = refs[:half], refs[half:]
     tile = others[0].shape[1]
+    copies = []
     for at in range(half):
         columns = slice(at * tile, (at + 1) * tile)
         value = jnp.dot(turned[...], rows[:, columns], preferred_element_type=F32)
         value = value + jnp.dot(turned_other[...], rows_other[:, columns], preferred_element_type=F32)
-        grads[:, columns] = (value + earlier[:, columns] + others[at][...].astype(F32)).astype(BF16)
-
-
-def finish_body(count, meta, ids, kept, arrived, combined, gate_grads):
+        store[at] = (value + earlier[:, columns] + others[at][...].astype(F32)).astype(BF16)
+        copies.append(pltpu.make_async_copy(store.at[at], grads.at[:, columns], sems.at[at]))
+        copies[-1].start()
+    for copy in copies:
+        copy.wait()
+
+
+def finish_body(count, meta, ids, kept, arrived, combined, gate_grads, token):
     width = combined.shape[1]
     combined[...] = (kept[:, :width] + arrived[:, :width].astype(F32)).astype(BF16)
     pieces = (kept[:, width:] + arrived[:, width:].astype(F32)).T
@@ -276,6 +348,7 @@
     for expert in range(count):
         found = found + jnp.where(named == expert, inner[expert : expert + 1, :], 0.0)
     gate_grads[...] = found
+    token[...] = jnp.zeros(token.shape, F32)
 
 
 def per_device(expert_ids, gates, hidden, weight, out_grad):
@@ -392,9 +465,7 @@
     for k in range(1, planes):
         lowest = k & -k
         if k != lowest:
-            forwarded = gathered[k ^ lowest]
-            forwarded = follow(forwarded, final_output) if relay else forwarded
-            gathered[k] = swap(forwarded, peers * lowest)
+            gathered[k] = swap(gathered[k ^ lowest], peers * lowest)
     if fold > 1:
         gathered = [jnp.concatenate(gathered[g * fold : (g + 1) * fold], 0) for g in range(groups)]
 
@@ -423,19 +494,18 @@
 
     jobs = [[(value, beside, at) for value in gathered] for at in (other_half, own_half)]
     if relay:
-        collected = call(
-            functools.partial(collect_body, planes), "collect", (1,),
-            [pl.BlockSpec((tokens, extent), beside)] * planes
-            + [pl.BlockSpec((tokens, large), other_half)] * planes
-            + [pl.BlockSpec((tokens, large), own_half)] * planes
-            + [glance],
-            [pl.BlockSpec((planes * tokens, large + extent), lambda i, m: (0, 0))] * 2,
-            [jax.ShapeDtypeStruct((planes * tokens, large + extent), BF16)] * 2,
-            meta, (*gathered * 3, final_output),
-            room=room,
+        beside_shape = jax.ShapeDtypeStruct((planes * tokens, large + extent), BF16)
+        collected = direct(
+            functools.partial(collect_body, planes), "collect", [beside_shape] * 2, meta, (*gathered, final_output),
         )
         near = [swap(value, 1 << number) for number, value in enumerate(collected)]
-        made = build_rows("own_rows", ((0, (0, 1)), (1, (1,)), (2, (0,))), jobs, (collected[0],))
+        plan = ((0, (0, 1)), (1, (1,)), (2, (0,)))
+        own_jobs = [[(k, 0, True) for k in range(planes)]] * 2
+        made = direct(
+            functools.partial(direct_rows_body, plan, own_jobs, planes, count), "own_rows",
+            [jax.ShapeDtypeStruct((len(parts) * rows, large), BF16) for _, parts in plan],
+            meta, (*gathered, collected[0]), scratch=[pltpu.VMEM((extent, tokens), F32)],
+        )
         arrived = [
             [(made[0], 0), (made[0], 1)], [None, (swap(made[1], 1), 0)], [(swap(made[2], 2), 0), None], [None, None],
         ]
@@ -474,6 +544,16 @@
             room=room,
         )
 
+    def direct_combine(chosen, dtype, after):
+        return direct(
+            functools.partial(direct_combine_body, peers, count, cap, tuple(chosen)), f"combine{chosen[0]}",
+            jax.ShapeDtypeStruct((len(chosen) * tokens, padded), dtype),
+            meta, (*[gathered[k] for k in chosen], after, *returned),
+            scratch=[pltpu.VMEM((extent, tokens), F32)],
+        )
+
+    if relay:
+        combine = direct_combine
     if fold == 1:
         leaving = combine(range(1, planes, 2), BF16, made[0])
         combine_done = combine(range(0, planes, 2), F32, leaving)
@@ -498,12 +578,13 @@
     summed = swap(leaving, peers * distance)
 
     if relay:
-        near_jobs = [
-            [(value, lambda i, m, k=k: (k, large // extent), lambda i, m, k=k: (k, 0)) for k in range(planes)]
-            for value in near
-        ]
         plan = ((0, (0,)), (2, (0,)), (0, (1,)), (1, (1,)))
-        made = build_rows("near_rows", plan, near_jobs, (combine_done,), NEAR_COST)
+        near_jobs = [[(job, k * tokens, False) for k in range(planes)] for job in range(2)]
+        made = direct(
+            functools.partial(direct_rows_body, plan, near_jobs, 2, count), "near_rows",
+            [jax.ShapeDtypeStruct((rows, large), BF16)] * 4,
+            meta, (*near, combine_done), scratch=[pltpu.VMEM((extent, tokens), F32)], cost=NEAR_COST,
+        )
         arrived[1][0], arrived[2][1] = (made[0], 0), (made[2], 0)
         arrived[3] = [(swap(made[1], 2), 0), (swap(made[3], 1), 0)]
 
@@ -547,22 +628,26 @@
     last_other, last_own = arrived[last]
     rows_own = last_own[0] if relay else last_own[0][rows:]
     rows_other = last_other[0] if relay else last_other[0][:rows]
-    followed = follow(rows_other, summed, last_own[0])
+
+    combined, gate_grads, finished = direct(
+        functools.partial(finish_body, count), "finish",
+        [
+            jax.ShapeDtypeStruct((tokens, width), BF16), jax.ShapeDtypeStruct((top, tokens), F32),
+            jax.ShapeDtypeStruct((16, 128), F32),
+        ],
+        meta, (ids_turned, sums[0], summed),
+    )
+    followed = follow(rows_other, finished, last_own[0])
     rows_other = exchange(followed)
-
-    combined, gate_grads = direct(
-        functools.partial(finish_body, count), "finish",
-        [jax.ShapeDtypeStruct((tokens, width), BF16), jax.ShapeDtypeStruct((top, tokens), F32)],
-        meta, (ids_turned, sums[0], summed),
-    )
-    hidden_grads, _ = inside_grad([last], hidden_grads, (followed,))
-    weight_grads = pl.pallas_call(
-        functools.partial(last_body, half, None),
-        name="last",
-        out_shape=jax.ShapeDtypeStruct((inside, large), BF16),
-        cost_estimate=pl.CostEstimate(flops=COST, bytes_accessed=COST, transcendentals=0),
-        compiler_params=pltpu.CompilerParams(vmem_limit_bytes=room * VMEM_BYTES),
-    )(turned_last, rows_own, turned_other, rows_other, total_own, *totals_other)
+    if relay:
+        arrived[last][0] = (followed, 0)
+    hidden_grads, _ = inside_grad([last], hidden_grads, ())
+    weight_grads = direct(
+        functools.partial(last_body, half), "last", jax.ShapeDtypeStruct((inside, large), BF16),
+        meta, (turned_last, rows_own, turned_other, rows_other, total_own, *totals_other),
+        out_specs=anywhere,
+        scratch=[pltpu.VMEM((half, inside, tile), BF16), pltpu.SemaphoreType.DMA((half,))],
+    )
 
     if fold > 1:
         hidden_grads = hidden_grads.reshape(peers, planes, cap, inside).transpose(1, 0, 2, 3)

time: 137 us -> 137 us (level)
  waiting for transfers between devices: 63.2 us -> 71 us
  starting transfers between devices: 22.9 us -> 17.9 us
  Pallas kernels: 46.2 us -> 43.5 us
    pallas_call x5 -> x11, Pallas kernels: 21.7 us -> 34.8 us  [direct(): pl.pallas_call(body, name=name, in_specs=[smem] + [places.get(at, vmem) f...]
    pallas_call x10 -> x5, Pallas kernels: 21.6 us -> 8.69 us  [call(): pl.pallas_call(body, name=name, grid_spec=pltpu.PrefetchScalarGridSpec(nu...]
    ppermute x14, waiting for transfers between devices: 61.7 us -> 71 us  [swap(): lax.ppermute(value, 'expert', [(e, e ^ distance) for e in range(count)])]
    ppermute x14, starting transfers between devices: 17.2 us -> 13.6 us  [swap(): lax.ppermute(value, 'expert', [(e, e ^ distance) for e in range(count)])]
    pallas_call x1 -> x0, Pallas kernels: 2.99 us -> none  [per_device(): pl.pallas_call(functools.partial(last_body, half, None), name='last', out...]
    ppermute x4, waiting for transfers between devices: 1.5 us -> 0.01 us  [exchange(): return lax.ppermute(value, 'dp', [(0, 1), (1, 0)])]
  transfers between devices with their start and end apart: 18 -> 18, of which waited for: 11 -> 7; matrix products, arithmetic and copies ran while one was open for 0% -> 0% of each run, Pallas kernels for 27% -> 24%
where the time goes in v1:
time: 137 us
  waiting for transfers between devices  71 us (52%)
  Pallas kernels  43.5 us (32%)
  starting transfers between devices  17.9 us (13%)
  local copies, waits for them, and re-layouts  3.49 us (3%)
    ppermute x14, waiting for transfers between devices, swap(): lax.ppermute(value, 'expert', [(e, e ^ distance) for e in range(count)])  71 us
    pallas_call x11, Pallas kernels, direct(): pl.pallas_call(body, name=name, in_specs=[smem] + [places.get(at, vmem) f...  34.8 us
    ppermute x14, starting transfers between devices, swap(): lax.ppermute(value, 'expert', [(e, e ^ distance) for e in range(count)])  13.6 us
    pallas_call x5, Pallas kernels, call(): pl.pallas_call(body, name=name, grid_spec=pltpu.PrefetchScalarGridSpec(nu...  8.69 us
    ppermute x4, starting transfers between devices, exchange(): return lax.ppermute(value, 'dp', [(0, 1), (1, 0)])  4.38 us
    unnamed x16, local copies, waits for them, and re-layouts  2.89 us
  transfers between devices with their start and end apart: 18, of which 7 were waited for; matrix products, arithmetic and copies ran while one was open for 0% of the time, Pallas kernels for 24%

profile of v1, /device:TPU:1, one launch (start us, length us, event | category | flops | bytes accessed | tf_op | source)
XLA Modules:
  0.0 137.2 jit_solution(1195509393291599376)
XLA Ops:
  1.3 6.7 %forward1.1 = (bf16[320,2048]{1,0:T(8,128)(2,1)}, bf16[320,2048]{1,0:T(8,128)(2,1)}) custom-call(s32[7]{0:T(128)} %stack.21.meta, bf16[4,4,80,768]{3,2,1,0:T(8,128)(2,1)} %bitcast.16, bf16[768,2048]{1,0:T(8,128)(2,1)} %bitcast.11), custom_call_target="tpu_custom_call" | custom-call | flops 1024 | bytes 1024 | tf_op jit(solution)/shard_map/forward1/pallas_call | solution.py:35
  8.0 2.1 %collective-permute-start.4 = (bf16[320,2048]{1,0:T(8,128)(2,1)}, bf16[320,2048]{1,0:T(8,128)(2,1)S(1)}, u32[]{:S(2)}, u32[]{:S(2)}) collective-permute-start(bf16[320,2048]{1,0:T(8,128)(2,1)} %get-tuple-element.28), channel_id=1, source_target_pairs={{0,2},{2,0},{4,6},{6,4},{8,10},{10,8},{12,14},{14,12},{16,18},{18,... | collective-permute-start | bytes 3932168 | tf_op jit(solution)/shard_map/ppermute | solution.py:382
  10.1 1.2 collective-permute-start.3
  11.3 0.8 pack.1.refs_3_.refs_0_
  12.2 2.4 %collective-permute-start = (bf16[128,2176]{1,0:T(8,128)(2,1)S(1)}, bf16[128,2176]{1,0:T(8,128)(2,1)S(1)}, u32[]{:S(2)}, u32[]{:S(2)}) collective-permute-start(bf16[128,2176]{1,0:T(8,128)(2,1)S(1)} %pack.1.refs_3_.refs_0_), channel_id=1, source_target_pairs={{0,16},{2,18},{4,20},{6,22},{8,24},{10,26},{12,28},{14,30},{16,0},... | collective-permute-start | bytes 1671176 | tf_op jit(solution)/shard_map/ppermute | solution.py:382
  14.6 1.3 collective-permute-start.1
  15.9 1.5 %copy-done.1 = bf16[1,1280,768]{2,1,0:T(8,128)(2,1)S(1)} copy-done((bf16[1,1280,768]{2,1,0:T(8,128)(2,1)S(1)}, bf16[1,1280,768]{2,1,0:T(8,128)(2,1)}, u32[]{:S(2)}) %copy-start.1) | copy-done | bytes 1966104
  17.4 1.3 copy-done.3
  18.7 2.6 %forward3.1.refs_2_.refs_0_ = bf16[320,2048]{1,0:T(8,128)(2,1)S(1)} custom-call(s32[7]{0:T(128)S(1)} %copy-done.5, bf16[4,4,80,768]{3,2,1,0:T(8,128)(2,1)S(1)} %bitcast.17, bf16[768,2048]{1,0:T(8,128)(2,1)S(1)} %bitcast.12, bf16[320,2048]{1,0:T(8,128)(2,1)S(1)} %copy-done.3, bf16[128,2176]{1,0:T(8,128)(2,1)S(1)} %pack.1.refs_3_.refs_0_), custom_call_target="tpu_custom_call" | custom-call | flops 1024 | bytes 1024 | tf_op jit(solution)/shard_map/forward3/pallas_call | solution.py:18
  21.4 2.6 %forward0.1.after.refs_3_ = bf16[320,2048]{1,0:T(8,128)(2,1)S(1)} custom-call(s32[7]{0:T(128)S(1)} %copy-done.5, bf16[4,4,80,768]{3,2,1,0:T(8,128)(2,1)S(1)} %bitcast.18, bf16[768,2048]{1,0:T(8,128)(2,1)S(1)} %bitcast.13, bf16[320,2048]{1,0:T(8,128)(2,1)S(1)} %forward3.1.refs_2_.refs_0_, bf16[128,2176]{1,0:T(8,128)(2,1)S(1)} %pack.1.refs_3_.refs_0_), custom_call_target="tpu_custom_call" | custom-call | flops 1024 | bytes 1024 | tf_op jit(solution)/shard_map/forward0/pallas_call | solution.py:18
  24.0 1.8 %turn.1 = (bf16[4,768,320]{2,1,0:T(8,128)(2,1)S(1)}, bf16[320,768]{1,0:T(8,128)(2,1)S(1)}, bf16[768,320]{1,0:T(8,128)(2,1)S(1)}) custom-call(s32[7]{0:T(128)S(1)} %copy-done.5, bf16[4,4,80,768]{3,2,1,0:T(8,128)(2,1)S(1)} %bitcast.19, bf16[320,2048]{1,0:T(8,128)(2,1)S(1)} %forward0.1.after.refs_3_), custom_call_target="tpu_custom_call" | custom-call | flops 1024 | bytes 1024 | tf_op jit(solution)/shard_map/turn/pallas_call | solution.py:18
  25.9 1.9 %collective-permute-start.5 = (bf16[320,768]{1,0:T(8,128)(2,1)S(1)}, bf16[320,768]{1,0:T(8,128)(2,1)S(1)}, u32[]{:S(2)}, u32[]{:S(2)}) collective-permute-start(bf16[320,768]{1,0:T(8,128)(2,1)S(1)} %get-tuple-element.29), channel_id=1, source_target_pairs={{0,1},{1,0},{2,3},{3,2},{4,5},{5,4},{6,7},{7,6},{8,9},{9,8},{10,11... | collective-permute-start | bytes 1474568 | tf_op jit(solution)/shard_map/ppermute | solution.py:385
  27.7 10.9 %collective-permute-done.refs_5_.refs_2_.refs_1_ = bf16[128,2176]{1,0:T(8,128)(2,1)S(1)} collective-permute-done((bf16[128,2176]{1,0:T(8,128)(2,1)S(1)}, bf16[128,2176]{1,0:T(8,128)(2,1)S(1)}, u32[]{:S(2)}, u32[]{:S(2)}) %collective-permute-start) | collective-permute-done | bytes 557088 | tf_op jit(solution)/shard_map/ppermute | solution.py:382
  38.6 1.4 %collective-permute-start.2 = (bf16[128,2176]{1,0:T(8,128)(2,1)S(1)}, bf16[128,2176]{1,0:T(8,128)(2,1)S(1)}, u32[]{:S(2)}, u32[]{:S(2)}) collective-permute-start(bf16[128,2176]{1,0:T(8,128)(2,1)S(1)} %collective-permute-done.refs_5_.refs_2_.refs_1_), channel_id=1, source_target_pairs={{0,8},{2,10},{4,12},{6,14},{8,0},{10,2},{12,4},{14,6},{16,24},{18,... | collective-permute-start | bytes 1671176 | tf_op jit(solution)/shard_map/ppermute | solution.py:382
  40.0 0.7 turn_other.1.refs_3_.turned_other
  41.1 10.4 %collective-permute-done.2.refs_3_.refs_1_ = bf16[128,2176]{1,0:T(8,128)(2,1)S(1)} collective-permute-done((bf16[128,2176]{1,0:T(8,128)(2,1)S(1)}, bf16[128,2176]{1,0:T(8,128)(2,1)S(1)}, u32[]{:S(2)}, u32[]{:S(2)}) %collective-permute-start.2) | collective-permute-done | bytes 557088 | tf_op jit(solution)/shard_map/ppermute | solution.py:382
  52.8 1.6 %own_rows.1 = (bf16[640,1024]{1,0:T(8,128)(2,1)S(1)}, bf16[320,1024]{1,0:T(8,128)(2,1)S(1)}, bf16[320,1024]{1,0:T(8,128)(2,1)S(1)}) custom-call(s32[7]{0:T(128)S(1)} %copy-done.5, bf16[128,2176]{1,0:T(8,128)(2,1)S(1)} %pack.1.refs_3_.refs_0_, bf16[128,2176]{1,0:T(8,128)(2,1)S(1)} %collective-permute-done.1.refs_4_.refs_1_.refs_0_, ...), custom_call_target="tpu_custom_call" | custom-call | flops 1024 | bytes 1024 | tf_op jit(solution)/shard_map/own_rows/pallas_call | solution.py:35
  54.5 16.9 %collective-permute-done.6.refs_6_ = bf16[320,2048]{1,0:T(8,128)(2,1)S(1)} collective-permute-done((bf16[320,2048]{1,0:T(8,128)(2,1)S(1)}, bf16[320,2048]{1,0:T(8,128)(2,1)S(1)}, u32[]{:S(2)}, u32[]{:S(2)}) %collective-permute-start.6) | collective-permute-done | bytes 1310752 | tf_op jit(solution)/shard_map/ppermute | solution.py:382
  71.4 2.9 %combine1.1.refs_2_ = bf16[256,2176]{1,0:T(8,128)(2,1)S(1)} custom-call(s32[7]{0:T(128)S(1)} %copy-done.5, bf16[128,2176]{1,0:T(8,128)(2,1)S(1)} %collective-permute-done.1.refs_4_.refs_1_.refs_0_, bf16[128,2176]{1,0:T(8,128)(2,1)S(1)} %collective-permute-done.2.refs_3_.refs_1_, bf16[640,1024]{1,0:T(8,128)(2,1)S(1)} %get-tuple-element.31.refs_2_.refs_0_, ...), custom_call_target="tpu_custom_call" | custom-call | flops 1024 | bytes 1024 | tf_op jit(solution)/shard_map/combine1/pallas_call | solution.py:35
  74.9 2.9 %combine0.1.refs_2_ = f32[256,2176]{1,0:T(8,128)S(1)} custom-call(s32[7]{0:T(128)S(1)} %copy-done.5, bf16[128,2176]{1,0:T(8,128)(2,1)S(1)} %pack.1.refs_3_.refs_0_, bf16[128,2176]{1,0:T(8,128)(2,1)S(1)} %collective-permute-done.refs_5_.refs_2_.refs_1_, bf16[256,2176]{1,0:T(8,128)(2,1)S(1)} %combine1.1.refs_2_, bf16[320,2048]{1,0:T(8,128)(2,1)S(1)} %forward0.1.after.refs_3_, ...), custom_call_target="tpu_custom_call" | custom-call | flops 1024 | bytes 1024 | tf_op jit(solution)/shard_map/combine0/pallas_call | solution.py:35
  77.8 20.0 %collective-permute-done.10.refs_1_ = bf16[512,1152]{1,0:T(8,128)(2,1)S(1)} collective-permute-done((bf16[512,1152]{1,0:T(8,128)(2,1)S(1)}, bf16[512,1152]{1,0:T(8,128)(2,1)S(1)}, u32[]{:S(2)}, u32[]{:S(2)}) %collective-permute-start.10) | collective-permute-done | bytes 1179680 | tf_op jit(solution)/shard_map/ppermute | solution.py:382
  97.8 1.7 %near_rows.1 = (bf16[320,1024]{1,0:T(8,128)(2,1)S(1)}, bf16[320,1024]{1,0:T(8,128)(2,1)S(1)}, bf16[320,1024]{1,0:T(8,128)(2,1)S(1)}, bf16[320,1024]{1,0:T(8,128)(2,1)S(1)}) custom-call(s32[7]{0:T(128)S(1)} %copy-done.5, bf16[512,1152]{1,0:T(8,128)(2,1)S(1)} %collective-permute-done.9.refs_0_, bf16[512,1152]{1,0:T(8,128)(2,1)S(1)} %collective-permute-done.10.refs_1_, ...), custom_call_target="tpu_custom_call" | custom-call | flops 10000000000 | bytes 1024 | tf_op jit(solution)/shard_map/near_rows/pallas_call | solution.py:35
  100.2 3.2 %collective-permute-start.8 = (bf16[128,2176]{1,0:T(8,128)(2,1)S(1)}, bf16[128,2176]{1,0:T(8,128)(2,1)S(1)}, u32[]{:S(2)}, u32[]{:S(2)}) collective-permute-start(bf16[128,2176]{1,0:T(8,128)(2,1)S(1)} %get-tuple-element.50), channel_id=1, source_target_pairs={{0,16},{2,18},{4,20},{6,22},{8,24},{10,26},{12,28},{14,30},{16,0},... | collective-permute-start | bytes 1671176 | tf_op jit(solution)/shard_map/ppermute | solution.py:382
  103.4 5.5 %collective-permute-done.13.refs_2_ = bf16[320,1024]{1,0:T(8,128)(2,1)S(1)} collective-permute-done((bf16[320,1024]{1,0:T(8,128)(2,1)S(1)}, bf16[320,1024]{1,0:T(8,128)(2,1)S(1)}, u32[]{:S(2)}, u32[]{:S(2)}) %collective-permute-start.13) | collective-permute-done | bytes 655392 | tf_op jit(solution)/shard_map/ppermute | solution.py:382
  108.8 3.0 %collective-permute-done.14.refs_3_ = bf16[320,1024]{1,0:T(8,128)(2,1)S(1)} collective-permute-done((bf16[320,1024]{1,0:T(8,128)(2,1)S(1)}, bf16[320,1024]{1,0:T(8,128)(2,1)S(1)}, u32[]{:S(2)}, u32[]{:S(2)}) %collective-permute-start.14) | collective-permute-done | bytes 655392 | tf_op jit(solution)/shard_map/ppermute | solution.py:382
  111.8 4.7 %inside0.1 = (bf16[4,4,80,768]{3,2,1,0:T(8,128)(2,1)}, f32[16,128]{1,0:T(8,128)S(1)}) custom-call(s32[7]{0:T(128)S(1)} %copy-done.5, bf16[768,2048]{1,0:T(8,128)(2,1)S(1)} %bitcast.14, bf16[640,1024]{1,0:T(8,128)(2,1)S(1)} %get-tuple-element.31.refs_2_.refs_0_, bf16[320,1024]{1,0:T(8,128)(2,1)S(1)} %get-tuple-element.38.refs_1_, ...), custom_call_target="tpu_custom_call" | custom-call | flops 1024 | bytes 1024 | tf_op jit(solution)/shard_map/inside0/pallas_call | solution.py:35
  116.5 5.6 %weight_grad.1 = (bf16[768,512]{1,0:T(8,128)(2,1)S(1)}, bf16[768,512]{1,0:T(8,128)(2,1)S(1)}, f32[768,1024]{1,0:T(8,128)S(1)}) custom-call(s32[7]{0:T(128)S(1)} %copy-done.5, bf16[4,768,320]{2,1,0:T(8,128)(2,1)S(1)} %get-tuple-element.45.turned, bf16[640,1024]{1,0:T(8,128)(2,1)S(1)} %get-tuple-element.31.refs_2_.refs_0_, ...), custom_call_target="tpu_custom_call" | custom-call | flops 1024 | bytes 1024 | tf_op jit(solution)/shard_map/weight_grad/pallas_call | solution.py:35
  122.0 1.8 %collective-permute-start.16 = (bf16[768,512]{1,0:T(8,128)(2,1)S(1)}, bf16[768,512]{1,0:T(8,128)(2,1)S(1)}, u32[]{:S(2)}, u32[]{:S(2)}) collective-permute-start(bf16[768,512]{1,0:T(8,128)(2,1)S(1)} %get-tuple-element.48), channel_id=1, source_target_pairs={{0,1},{1,0},{2,3},{3,2},{4,5},{5,4},{6,7},{7,6},{8,9},{9,8},{10,11... | collective-permute-start | bytes 2359304 | tf_op jit(solution)/shard_map/ppermute | solution.py:385
  123.9 4.4 %collective-permute-done.8.arrived = bf16[128,2176]{1,0:T(8,128)(2,1)S(1)} collective-permute-done((bf16[128,2176]{1,0:T(8,128)(2,1)S(1)}, bf16[128,2176]{1,0:T(8,128)(2,1)S(1)}, u32[]{:S(2)}, u32[]{:S(2)}) %collective-permute-start.8) | collective-permute-done | bytes 557088 | tf_op jit(solution)/shard_map/ppermute | solution.py:382
  128.3 1.6 %finish.1 = (bf16[128,2048]{1,0:T(8,128)(2,1)}, f32[8,128]{1,0:T(8,128)}, f32[16,128]{1,0:T(8,128)S(1)}) custom-call(s32[7]{0:T(128)S(1)} %copy-done.5, s32[8,128]{1,0:T(8,128)S(1)} %bitcast.21, f32[128,2176]{1,0:T(8,128)S(1)} %get-tuple-element.51.kept, bf16[128,2176]{1,0:T(8,128)(2,1)S(1)} %collective-permute-done.8.arrived), custom_call_target="tpu_custom_call" | custom-call | flops 1024 | bytes 1024 | tf_op jit(solution)/shard_map/finish/pallas_call | solution.py:35
  130.5 3.1 %inside3.1 = (bf16[4,4,80,768]{3,2,1,0:T(8,128)(2,1)}, f32[16,128]{1,0:T(8,128)}) custom-call(s32[7]{0:T(128)S(1)} %copy-done.5, bf16[768,2048]{1,0:T(8,128)(2,1)S(1)} %bitcast.15, bf16[320,1024]{1,0:T(8,128)(2,1)S(1)} %follow.3.refs_0_, bf16[320,1024]{1,0:T(8,128)(2,1)S(1)} %collective-permute-done.12.refs_2_.refs_1_.rows, ...), custom_call_target="tpu_custom_call", output_to_operand_aliasing={{0}: (4, {})} | custom-call | flops 1024 | bytes 1024 | tf_op jit(solution)/shard_map/inside3/pallas_call | solution.py:35
  133.7 3.3 %last.1 = bf16[768,1024]{1,0:T(8,128)(2,1)} custom-call(s32[7]{0:T(128)S(1)} %copy-done.5, bf16[768,320]{1,0:T(8,128)(2,1)S(1)} %get-tuple-element.44.turned, bf16[320,1024]{1,0:T(8,128)(2,1)S(1)} %collective-permute-done.12.refs_2_.refs_1_.rows, bf16[768,320]{1,0:T(8,128)(2,1)S(1)} %turn_other.1.refs_3_.turned_other, ...), custom_call_target="tpu_custom_call" | custom-call | flops 1024 | bytes 1024 | tf_op jit(solution)/shard_map/last/pallas_call | solution.py:35
  (42 shorter events, 4.2 us)
Async XLA Ops:
  1.2 10.1 %copy-start.4 = (bf16[128,2048]{1,0:T(8,128)(2,1)S(1)}, bf16[128,2048]{1,0:T(8,128)(2,1)}, u32[]{:S(2)}) copy-start(bf16[128,2048]{1,0:T(8,128)(2,1)} %grad.1) | copy-start | bytes 1572868
  1.2 10.1 %copy-start.5 = (s32[7]{0:T(128)S(1)}, s32[7]{0:T(128)}, u32[]{:S(2)}) copy-start(s32[7]{0:T(128)} %stack.21.meta) | copy-start | bytes 88
  1.3 10.1 %copy-start.6 = (s32[128,8]{0,1:T(8,128)S(1)}, s32[128,8]{0,1:T(8,128)}, u32[]{:S(2)}) copy-start(s32[128,8]{0,1:T(8,128)} %param.5) | copy-start | bytes 12292
  1.3 10.1 %copy-start.7 = (f32[128,8]{0,1:T(8,128)S(1)}, f32[128,8]{0,1:T(8,128)}, u32[]{:S(2)}) copy-start(f32[128,8]{0,1:T(8,128)} %param.6) | copy-start | bytes 12292
  1.3 14.6 %copy-start = (bf16[1,768,2048]{2,1,0:T(8,128)(2,1)S(1)}, bf16[1,768,2048]{2,1,0:T(8,128)(2,1)}, u32[]{:S(2)}) copy-start(bf16[1,768,2048]{2,1,0:T(8,128)(2,1)} %param.8) | copy-start | bytes 9437188
  8.0 32.8 %collective-permute-start.4 = (bf16[320,2048]{1,0:T(8,128)(2,1)}, bf16[320,2048]{1,0:T(8,128)(2,1)S(1)}, u32[]{:S(2)}, u32[]{:S(2)}) collective-permute-start(bf16[320,2048]{1,0:T(8,128)(2,1)} %get-tuple-element.28), channel_id=1, source_target_pairs={{0,2},{2,0},{4,6},{6,4},{8,10},{10,8},{12,14},{14,12},{16,18},{18,... | collective-permute-start | bytes 3932168 | tf_op jit(solution)/shard_map/ppermute | solution.py:382
  10.1 30.7 %collective-permute-start.3 = (bf16[320,2048]{1,0:T(8,128)(2,1)}, bf16[320,2048]{1,0:T(8,128)(2,1)S(1)}, u32[]{:S(2)}, u32[]{:S(2)}) collective-permute-start(bf16[320,2048]{1,0:T(8,128)(2,1)} %get-tuple-element.27.refs_2_), channel_id=1, source_target_pairs={{0,4},{2,6},{4,0},{6,2},{8,12},{10,14},{12,8},{14,10},{16,20},{18,... | collective-permute-start | bytes 3932168 | tf_op jit(solution)/shard_map/ppermute | solution.py:382
  12.2 26.4 %collective-permute-start = (bf16[128,2176]{1,0:T(8,128)(2,1)S(1)}, bf16[128,2176]{1,0:T(8,128)(2,1)S(1)}, u32[]{:S(2)}, u32[]{:S(2)}) collective-permute-start(bf16[128,2176]{1,0:T(8,128)(2,1)S(1)} %pack.1.refs_3_.refs_0_), channel_id=1, source_target_pairs={{0,16},{2,18},{4,20},{6,22},{8,24},{10,26},{12,28},{14,30},{16,0},... | collective-permute-start | bytes 1671176 | tf_op jit(solution)/shard_map/ppermute | solution.py:382
  14.6 26.2 %collective-permute-start.1 = (bf16[128,2176]{1,0:T(8,128)(2,1)S(1)}, bf16[128,2176]{1,0:T(8,128)(2,1)S(1)}, u32[]{:S(2)}, u32[]{:S(2)}) collective-permute-start(bf16[128,2176]{1,0:T(8,128)(2,1)S(1)} %pack.1.refs_3_.refs_0_), channel_id=1, source_target_pairs={{0,8},{2,10},{4,12},{6,14},{8,0},{10,2},{12,4},{14,6},{16,24},{18,... | collective-permute-start | bytes 1671176 | tf_op jit(solution)/shard_map/ppermute | solution.py:382
  15.9 1.5 %copy-start.1 = (bf16[1,1280,768]{2,1,0:T(8,128)(2,1)S(1)}, bf16[1,1280,768]{2,1,0:T(8,128)(2,1)}, u32[]{:S(2)}) copy-start(bf16[1,1280,768]{2,1,0:T(8,128)(2,1)} %param.7) | copy-start | bytes 5898244
  17.4 1.3 copy-start.3
  21.4 2.7 %copy-start.2 = (bf16[1,1280,768]{2,1,0:T(8,128)(2,1)S(1)}, bf16[1,1280,768]{2,1,0:T(8,128)(2,1)}, u32[]{:S(2)}) copy-start(bf16[1,1280,768]{2,1,0:T(8,128)(2,1)} %param.7) | copy-start | bytes 5898244
  25.9 14.1 %collective-permute-start.5 = (bf16[320,768]{1,0:T(8,128)(2,1)S(1)}, bf16[320,768]{1,0:T(8,128)(2,1)S(1)}, u32[]{:S(2)}, u32[]{:S(2)}) collective-permute-start(bf16[320,768]{1,0:T(8,128)(2,1)S(1)} %get-tuple-element.29), channel_id=1, source_target_pairs={{0,1},{1,0},{2,3},{3,2},{4,5},{5,4},{6,7},{7,6},{8,9},{9,8},{10,11... | collective-permute-start | bytes 1474568 | tf_op jit(solution)/shard_map/ppermute | solution.py:385
  38.6 12.9 %collective-permute-start.2 = (bf16[128,2176]{1,0:T(8,128)(2,1)S(1)}, bf16[128,2176]{1,0:T(8,128)(2,1)S(1)}, u32[]{:S(2)}, u32[]{:S(2)}) collective-permute-start(bf16[128,2176]{1,0:T(8,128)(2,1)S(1)} %collective-permute-done.refs_5_.refs_2_.refs_1_), channel_id=1, source_target_pairs={{0,8},{2,10},{4,12},{6,14},{8,0},{10,2},{12,4},{14,6},{16,24},{18,... | collective-permute-start | bytes 1671176 | tf_op jit(solution)/shard_map/ppermute | solution.py:382
  40.8 30.5 %collective-permute-start.6 = (bf16[320,2048]{1,0:T(8,128)(2,1)S(1)}, bf16[320,2048]{1,0:T(8,128)(2,1)S(1)}, u32[]{:S(2)}, u32[]{:S(2)}) collective-permute-start(bf16[320,2048]{1,0:T(8,128)(2,1)S(1)} %follow.2.refs_4_), channel_id=1, source_target_pairs={{0,6},{2,4},{4,2},{6,0},{8,14},{10,12},{12,10},{14,8},{16,22},{18,... | collective-permute-start | bytes 3932168 | tf_op jit(solution)/shard_map/ppermute | solution.py:382
  52.2 45.5 %collective-permute-start.10 = (bf16[512,1152]{1,0:T(8,128)(2,1)S(1)}, bf16[512,1152]{1,0:T(8,128)(2,1)S(1)}, u32[]{:S(2)}, u32[]{:S(2)}) collective-permute-start(bf16[512,1152]{1,0:T(8,128)(2,1)S(1)} %get-tuple-element.34), channel_id=1, source_target_pairs={{0,4},{2,6},{4,0},{6,2},{8,12},{10,14},{12,8},{14,10},{16,20},{18,... | collective-permute-start | bytes 3538952 | tf_op jit(solution)/shard_map/ppermute | solution.py:382
  52.5 45.2 %collective-permute-start.9 = (bf16[512,1152]{1,0:T(8,128)(2,1)S(1)}, bf16[512,1152]{1,0:T(8,128)(2,1)S(1)}, u32[]{:S(2)}, u32[]{:S(2)}) collective-permute-start(bf16[512,1152]{1,0:T(8,128)(2,1)S(1)} %get-tuple-element.30.refs_4_), channel_id=1, source_target_pairs={{0,2},{2,0},{4,6},{6,4},{8,10},{10,8},{12,14},{14,12},{16,18},{18,... | collective-permute-start | bytes 3538952 | tf_op jit(solution)/shard_map/ppermute | solution.py:382
  74.3 25.7 %collective-permute-start.7 = (bf16[256,2176]{1,0:T(8,128)(2,1)S(1)}, bf16[256,2176]{1,0:T(8,128)(2,1)S(1)}, u32[]{:S(2)}, u32[]{:S(2)}) collective-permute-start(bf16[256,2176]{1,0:T(8,128)(2,1)S(1)} %combine1.1.refs_2_), channel_id=1, source_target_pairs={{0,8},{2,10},{4,12},{6,14},{8,0},{10,2},{12,4},{14,6},{16,24},{18,... | collective-permute-start | bytes 3342344 | tf_op jit(solution)/shard_map/ppermute | solution.py:382
  74.3 34.5 %collective-permute-start.13 = (bf16[320,1024]{1,0:T(8,128)(2,1)S(1)}, bf16[320,1024]{1,0:T(8,128)(2,1)S(1)}, u32[]{:S(2)}, u32[]{:S(2)}) collective-permute-start(bf16[320,1024]{1,0:T(8,128)(2,1)S(1)} %get-tuple-element.39), channel_id=1, source_target_pairs={{0,2},{2,0},{4,6},{6,4},{8,10},{10,8},{12,14},{14,12},{16,18},{18,... | collective-permute-start | bytes 1966088 | tf_op jit(solution)/shard_map/ppermute | solution.py:382
  74.7 37.1 %collective-permute-start.14 = (bf16[320,1024]{1,0:T(8,128)(2,1)S(1)}, bf16[320,1024]{1,0:T(8,128)(2,1)S(1)}, u32[]{:S(2)}, u32[]{:S(2)}) collective-permute-start(bf16[320,1024]{1,0:T(8,128)(2,1)S(1)} %get-tuple-element.40), channel_id=1, source_target_pairs={{0,4},{2,6},{4,0},{6,2},{8,12},{10,14},{12,8},{14,10},{16,20},{18,... | collective-permute-start | bytes 1966088 | tf_op jit(solution)/shard_map/ppermute | solution.py:382
  99.5 30.4 %collective-permute-start.12 = (bf16[320,1024]{1,0:T(8,128)(2,1)S(1)}, bf16[320,1024]{1,0:T(8,128)(2,1)S(1)}, u32[]{:S(2)}, u32[]{:S(2)}) collective-permute-start(bf16[320,1024]{1,0:T(8,128)(2,1)S(1)} %get-tuple-element.37), channel_id=1, source_target_pairs={{0,2},{2,0},{4,6},{6,4},{8,10},{10,8},{12,14},{14,12},{16,18},{18,... | collective-permute-start | bytes 1966088 | tf_op jit(solution)/shard_map/ppermute | solution.py:382
  99.8 30.1 %collective-permute-start.11 = (bf16[320,1024]{1,0:T(8,128)(2,1)S(1)}, bf16[320,1024]{1,0:T(8,128)(2,1)S(1)}, u32[]{:S(2)}, u32[]{:S(2)}) collective-permute-start(bf16[320,1024]{1,0:T(8,128)(2,1)S(1)} %get-tuple-element.35), channel_id=1, source_target_pairs={{0,4},{2,6},{4,0},{6,2},{8,12},{10,14},{12,8},{14,10},{16,20},{18,... | collective-permute-start | bytes 1966088 | tf_op jit(solution)/shard_map/ppermute | solution.py:382
  100.2 28.1 %collective-permute-start.8 = (bf16[128,2176]{1,0:T(8,128)(2,1)S(1)}, bf16[128,2176]{1,0:T(8,128)(2,1)S(1)}, u32[]{:S(2)}, u32[]{:S(2)}) collective-permute-start(bf16[128,2176]{1,0:T(8,128)(2,1)S(1)} %get-tuple-element.50), channel_id=1, source_target_pairs={{0,16},{2,18},{4,20},{6,22},{8,24},{10,26},{12,28},{14,30},{16,0},... | collective-permute-start | bytes 1671176 | tf_op jit(solution)/shard_map/ppermute | solution.py:382
  122.0 11.7 %collective-permute-start.16 = (bf16[768,512]{1,0:T(8,128)(2,1)S(1)}, bf16[768,512]{1,0:T(8,128)(2,1)S(1)}, u32[]{:S(2)}, u32[]{:S(2)}) collective-permute-start(bf16[768,512]{1,0:T(8,128)(2,1)S(1)} %get-tuple-element.48), channel_id=1, source_target_pairs={{0,1},{1,0},{2,3},{3,2},{4,5},{5,4},{6,7},{7,6},{8,9},{9,8},{10,11... | collective-permute-start | bytes 2359304 | tf_op jit(solution)/shard_map/ppermute | solution.py:385
  123.8 9.9 %collective-permute-start.17 = (bf16[768,512]{1,0:T(8,128)(2,1)S(1)}, bf16[768,512]{1,0:T(8,128)(2,1)S(1)}, u32[]{:S(2)}, u32[]{:S(2)}) collective-permute-start(bf16[768,512]{1,0:T(8,128)(2,1)S(1)} %get-tuple-element.49), channel_id=1, source_target_pairs={{0,1},{1,0},{2,3},{3,2},{4,5},{5,4},{6,7},{7,6},{8,9},{9,8},{10,11... | collective-permute-start | bytes 2359304 | tf_op jit(solution)/shard_map/ppermute | solution.py:385
  129.9 3.8 %collective-permute-start.15 = (bf16[320,1024]{1,0:T(8,128)(2,1)S(1)}, bf16[320,1024]{1,0:T(8,128)(2,1)S(1)}, u32[]{:S(2)}, u32[]{:S(2)}) collective-permute-start(bf16[320,1024]{1,0:T(8,128)(2,1)S(1)} %follow.3.refs_0_), channel_id=1, source_target_pairs={{0,1},{1,0},{2,3},{3,2},{4,5},{5,4},{6,7},{7,6},{8,9},{9,8},{10,11... | collective-permute-start | bytes 1966088 | tf_op jit(solution)/shard_map/ppermute | solution.py:385
